TPU v7x, 512 devices: a whole 4x4x16 slice. The times are simulated.
512 devices in a mesh: ia: 32 (over z, core), ja: 4 (over y), ka: 4 (over x).
Axes of the slice: x: 4, y: 4, z: 16, core: 2. Of those that a mesh axis runs over, the one named last changes fastest.
Arguments:
- tensor: float32 [512, 1024, 512], P('ia', 'ja', 'ka'), may hold values from -75 to 75
- second_factor: float32 [4, 256, 24], P('ja', 'ia'), may hold values from -0.79549513 to 0.79549513
- third_factor: float32 [4, 128, 24], P('ka', 'ia'), may hold values from -1.125 to 1.125
Outputs:
- factor: float32 [512, 24], P('ia')
- column_rms: float32 [24], replicated
- correlation: float32 [24, 24], replicated
All inputs are finite; a program needn't handle non-finite values.
Results may differ from a plain program's by a relative error of at most 0.0003.
Values sent between devices are 32-bit elements; how exact they have to be, the bound alone decides.
No kernel may reach another device: no remote copies, remote signals or barrier semaphores. Data moves between devices by JAX's collectives and lax.ppermute only.
A program may use at most 64 MiB of HBM per device.

v0:
```python
import jax
import jax.numpy as jnp
from jax import lax
from jax.sharding import PartitionSpec as P

EPSILON = 1e-06


def gram_of(row_block):
    return jnp.dot(
        row_block.T, row_block, precision=lax.Precision.HIGHEST, preferred_element_type=jnp.float32
    )


def solve_rows(system, row_block):
    lower_factor = jnp.linalg.cholesky(system)
    return jax.scipy.linalg.cho_solve((lower_factor, True), row_block.T).T


def per_device(tensor, second_factor, third_factor):
    highest = lax.Precision.HIGHEST
    width_rank = second_factor.shape[-1]
    block_two, block_three = (
        lax.all_gather(second_factor, "ia", axis=1, tiled=True),
        lax.all_gather(third_factor, "ia", axis=1, tiled=True),
    )
    rows_two = block_two[0]
    rows_three = block_three[0]
    paired = (rows_two.T[:, :, None] * rows_three.T[:, None, :]).reshape(width_rank, -1)
    local_rows = tensor.shape[0]
    total_rows = local_rows * lax.axis_size("ia")
    gram_two = lax.psum(gram_of(rows_two), "ja")
    gram_three = lax.psum(gram_of(rows_three), "ka")
    system = gram_two * gram_three
    flattened = tensor.reshape(tensor.shape[0], -1)
    summed = lax.psum(
        lax.dot_general(
            flattened,
            paired,
            (((1,), (1,)), ((), ())),
            precision=highest,
            preferred_element_type=jnp.float32,
        ),
        ("ja", "ka"),
    )
    updated = solve_rows(system, summed)
    gram_first = lax.psum(gram_of(updated), "ia")
    column_rms = jnp.sqrt(jnp.diagonal(gram_first) / total_rows + EPSILON)
    factor = updated / column_rms[None, :]
    correlation = gram_first / (column_rms[:, None] * column_rms[None, :]) / total_rows
    return (factor, column_rms, correlation)


def solution(mesh):
    return jax.shard_map(
        per_device,
        mesh=mesh,
        in_specs=(P("ia", "ja", "ka"), P("ja", "ia", None), P("ka", "ia", None)),
        out_specs=(P("ia", None), P(), P()),
        check_vma=False,
    )
```

profile of v0, /device:TPU:1, one launch (start us, length us, event | category | flops | bytes accessed | tf_op | source)
XLA Modules:
  0.0 234.9 jit_solution(12717205407412685473)
XLA Ops:
  0.6 0.0 copy-start
  0.7 38.1 %all_gather.7 = f32[1,128,24]{2,0,1:T(1,128)S(1)} all-gather(f32[1,4,24]{2,0,1:T(1,128)} %bitcast.37), channel_id=1, replica_groups=mesh['ia'=32,'ja'=4,'ka'=4] {'ia'}, dimensions={1}, use_global_device_ids=true | all-gather | bytes 12672 | tf_op jit(solution)/shard_map/all_gather | solution.py:25
  38.8 0.2 fusion.18
  39.0 13.1 %psum.29 = f32[24,24]{0,1:T(8,128)S(1)} all-reduce(f32[24,24]{0,1:T(8,128)S(1)} %fusion.18), channel_id=1, replica_groups=mesh['ia'=32,'ja'=4,'ka'=4] {'ka'}, use_global_device_ids=true, to_apply=%region_1.0 | all-reduce | flops 576 | bytes 4608 | tf_op jit(solution)/shard_map/psum | solution.py:33
  52.1 0.1 copy.20
  52.2 31.2 %all_gather.6 = f32[1,256,24]{2,1,0:T(8,128)S(1)} all-gather(f32[1,8,24]{2,1,0:T(8,128)} %param.4), channel_id=1, replica_groups=mesh['ia'=32,'ja'=4,'ka'=4] {'ia'}, dimensions={1}, use_global_device_ids=true | all-gather | bytes 25344 | tf_op jit(solution)/shard_map/all_gather | solution.py:24
  83.4 0.0 copy-done
  83.4 4.0 %fusion.5 = f32[16,24]{1,0:T(8,128)S(1)} fusion(f32[16,256,128]{2,1,0:T(8,128)S(1)} %copy-done, f32[24,128]{1,0:T(8,128)S(1)} %copy.20, f32[24,256]{0,1:T(8,128)S(1)} %bitcast.34), kind=kOutput, calls=%fused_computation.6 | convolution fusion | flops 151781376 | bytes 2135552 | tf_op jit(solution)/shard_map/dot_general | solution.py:37
  87.4 30.9 %psum.30 = f32[16,24]{1,0:T(8,128)S(1)} all-reduce(f32[16,24]{1,0:T(8,128)S(1)} %fusion.5), channel_id=1, replica_groups=mesh['ia'=32,'ja'=4,'ka'=4] {'ja','ka'}, use_global_device_ids=true, to_apply=%region_4.5 | all-reduce | flops 384 | bytes 3072 | tf_op jit(solution)/shard_map/psum | solution.py:36
  118.3 0.3 fusion.10
  118.7 11.1 %psum.28 = f32[24,24]{0,1:T(8,128)S(1)} all-reduce(f32[24,24]{0,1:T(8,128)S(1)} %fusion.10), channel_id=1, replica_groups=mesh['ia'=32,'ja'=4,'ka'=4] {'ja'}, use_global_device_ids=true, to_apply=%region_0.0 | all-reduce | flops 576 | bytes 4608 | tf_op jit(solution)/shard_map/psum | solution.py:32
  129.8 0.1 copy.19
  129.8 2.2 cholesky.16
  132.1 0.6 compare_reduce_fusion
  132.7 0.6 fusion.12
  133.4 1.8 custom-call.10
  135.2 0.1 fusion.15
  135.3 0.1 fusion.13
  135.5 0.2 fusion.19
  135.7 97.1 %psum.31 = f32[24,24]{1,0:T(8,128)S(1)} all-reduce(f32[24,24]{1,0:T(8,128)S(1)} %fusion.19), channel_id=1, replica_groups=mesh['ia'=32,'ja'=4,'ka'=4] {'ia'}, use_global_device_ids=true, to_apply=%region_5.6 | all-reduce | flops 576 | bytes 4608 | tf_op jit(solution)/shard_map/psum | solution.py:47
  232.8 0.8 gather_fusion
  233.6 0.0 copy-start.1
  233.6 0.7 divide_multiply_fusion
  234.3 0.6 divide_bitcast_fusion
  234.9 0.0 copy-done.1
  (5 shorter events, 0.1 us)
Async XLA Ops:
  0.6 82.8 %copy-start = (f32[16,256,128]{2,1,0:T(8,128)S(1)}, f32[16,256,128]{2,1,0:T(8,128)}, u32[]{:S(2)}) copy-start(f32[16,256,128]{2,1,0:T(8,128)} %param.3) | copy-start | bytes 6291460
  233.6 1.3 copy-start.1
where the time goes:
time: 236 us; the launch traced here: 235 us
  blocking collectives  222 us (94%)
  other arithmetic  6.67 us (3%)
  matrix products  5.09 us (2%)
    psum x1, blocking collectives, per_device(): gram_first = lax.psum(gram_of(updated), 'ia')  97.1 us
    all_gather x1, blocking collectives, per_device(): lax.all_gather(third_factor, 'ia', axis=1, tiled=True)  38.1 us
    all_gather x1, blocking collectives, per_device(): lax.all_gather(second_factor, 'ia', axis=1, tiled=True)  31.2 us
    psum x1, blocking collectives, per_device(): lax.psum(lax.dot_general(flattened, paired, (((1,), (1,)), ((), ())), pre...  30.9 us
    psum x1, blocking collectives, per_device(): gram_three = lax.psum(gram_of(rows_three), 'ka')  13.1 us
    psum x1, blocking collectives, per_device(): gram_two = lax.psum(gram_of(rows_two), 'ja')  11.1 us

commit v1 on v0

v1 whole, which is shorter than its diff:
```python
import jax
import jax.numpy as jnp
from jax import lax
from jax.sharding import PartitionSpec as P

EPSILON = 1e-06


def gram_of(row_block):
    return jnp.dot(
        row_block.T, row_block, precision=lax.Precision.HIGHEST, preferred_element_type=jnp.float32
    )


def solve_rows(system, row_block):
    lower_factor = jnp.linalg.cholesky(system)
    return jax.scipy.linalg.cho_solve((lower_factor, True), row_block.T).T


def exchange(flat, axes):
    count = lax.axis_size(axes)
    return lax.all_to_all(jnp.broadcast_to(flat[None], (count,) + flat.shape), axes, 0, 0, tiled=True)


def per_device(tensor, second_factor, third_factor):
    highest = lax.Precision.HIGHEST
    rank = second_factor.shape[-1]
    own_two, own_three = second_factor[0], third_factor[0]
    local_rows = tensor.shape[0]
    total_rows = local_rows * lax.axis_size("ia")

    packed = jnp.concatenate([own_two.reshape(-1), own_three.reshape(-1)])
    gathered = exchange(packed, "ia")
    rows_two = gathered[:, : own_two.size].reshape(-1, rank)
    rows_three = gathered[:, own_two.size :].reshape(-1, rank)

    through = jnp.einsum(
        "ijk,kr->ijr", tensor, rows_three, precision=highest, preferred_element_type=jnp.float32
    )
    partial = jnp.sum(through * rows_two[None], axis=1)
    message = jnp.concatenate([partial, gram_of(rows_two), gram_of(rows_three)], axis=0)
    parts = exchange(message.reshape(-1), ("ja", "ka"))
    scale_two, scale_three = 1.0 / lax.axis_size("ka"), 1.0 / lax.axis_size("ja")
    total = jnp.sum(parts, axis=0).reshape(-1, rank)
    summed = total[:local_rows]
    gram_two = total[local_rows : local_rows + rank] * scale_two
    gram_three = total[local_rows + rank :] * scale_three
    updated = solve_rows(gram_two * gram_three, summed)

    grams = exchange(gram_of(updated).reshape(-1), "ia")
    gram_first = jnp.sum(grams, axis=0).reshape(rank, rank)
    column_rms = jnp.sqrt(jnp.diagonal(gram_first) / total_rows + EPSILON)
    factor = updated / column_rms[None, :]
    correlation = gram_first / (column_rms[:, None] * column_rms[None, :]) / total_rows
    return (factor, column_rms, correlation)


def solution(mesh):
    return jax.shard_map(
        per_device,
        mesh=mesh,
        in_specs=(P("ia", "ja", "ka"), P("ja", "ia", None), P("ka", "ia", None)),
        out_specs=(P("ia", None), P(), P()),
        check_vma=False,
    )
```

time: 236 us -> 77.8 us (0.33)
  blocking collectives: 222 us -> 42.3 us
  waiting for transfers between devices: 0 us -> 13.8 us
  starting transfers between devices: 0 us -> 6.39 us
  local copies, waits for them, and re-layouts: 0.92 us -> 4.25 us
    psum x4 -> x0, blocking collectives: 152 us -> none  [the longest x1 97.1 us: per_device(): gram_first = lax.psum(gram_of(updated), 'ia')]
    all_gather x2 -> x0, blocking collectives: 69.3 us -> none  [the longest x1 38.1 us: per_device(): lax.all_gather(third_factor, 'ia', axis=1, tiled=True)]
    all_to_all x0 -> x2, blocking collectives: none -> 42.3 us  [exchange(): lax.all_to_all(jnp.broadcast_to(flat[None], (count,) + flat.shape), axes,...]
    all_to_all x0 -> x1, waiting for transfers between devices: none -> 13.8 us  [exchange(): lax.all_to_all(jnp.broadcast_to(flat[None], (count,) + flat.shape), axes,...]
    all_to_all x0 -> x1, starting transfers between devices: none -> 6.39 us  [exchange(): lax.all_to_all(jnp.broadcast_to(flat[None], (count,) + flat.shape), axes,...]
  transfers between devices with their start and end apart: 0 -> 1, of which waited for: 0 -> 1; matrix products, arithmetic and copies ran while one was open for 0% -> 0% of each run, Pallas kernels for 0% -> 0%
where the time goes in v1:
time: 77.8 us; the launch traced here: 77.5 us
  blocking collectives  42.3 us (54%)
  waiting for transfers between devices  13.8 us (18%)
  other arithmetic  7.04 us (9%)
  starting transfers between devices  6.39 us (8%)
  local copies, waits for them, and re-layouts  4.25 us (5%)
  matrix products  3.03 us (4%)
    all_to_all x2, blocking collectives, exchange(): lax.all_to_all(jnp.broadcast_to(flat[None], (count,) + flat.shape), axes,...  42.3 us
    all_to_all x1, waiting for transfers between devices, exchange(): lax.all_to_all(jnp.broadcast_to(flat[None], (count,) + flat.shape), axes,...  13.8 us
    all_to_all x1, starting transfers between devices, exchange(): lax.all_to_all(jnp.broadcast_to(flat[None], (count,) + flat.shape), axes,...  6.39 us
    another operation x3, other arithmetic, solve_rows(): lower_factor = jnp.linalg.cholesky(system)  2.87 us
    another operation x2, other arithmetic, solve_rows(): return jax.scipy.linalg.cho_solve((lower_factor, True), row_block.T).T  2.48 us
    dot_general x1, matrix products, per_device(): jnp.einsum('ijk,kr->ijr', tensor, rows_three, precision=highest, preferre...  1.94 us
    another operation x2, local copies, waits for them, and re-layouts, per_device(): packed = jnp.concatenate([own_two.reshape(-1), own_three.reshape(-1)])  1.68 us
  transfers between devices with their start and end apart: 1, of which 1 were waited for; matrix products, arithmetic and copies ran while one was open for 0% of the time, Pallas kernels for 0%

profile of v1, /device:TPU:1, one launch (start us, length us, event | category | flops | bytes accessed | tf_op | source)
XLA Modules:
  0.0 77.5 jit_solution(16218026620484762940)
XLA Ops:
  0.6 0.9 %reshape_squeeze.6 = f32[192]{0:T(256)S(1)} reshape(f32[1,8,24]{2,1,0:T(8,128)} %param.4) | data formatting | bytes 1536 | tf_op jit(solution)/shard_map/reshape;squeeze | solution.py:32
  1.6 0.8 reshape_squeeze.7
  2.3 0.1 pad_maximum_fusion.1
  2.4 29.0 %all_to_all.21 = f32[32,1,288]{2,1,0:T(1,128)S(1)} all-to-all(f32[32,1,288]{2,1,0:T(1,128)S(1)} %broadcast_in_dim.16), channel_id=1, replica_groups=mesh['ia'=32,'ja'=4,'ka'=4] {'ia'}, dimensions={0} | all-to-all | bytes 73728 | tf_op jit(solution)/shard_map/all_to_all | solution.py:22
  31.6 0.1 mul.37
  31.7 0.4 fusion.10
  32.1 0.1 reshape.92
  32.2 0.2 fusion.11
  32.5 1.9 %fusion.1 = f32[16,24]{1,0:T(8,128)S(1)} fusion(f32[16,256,128]{2,1,0:T(8,128)S(1)} %copy-done, f32[256,24]{0,1:T(8,128)S(1)} %copy.22, f32[128,24]{1,0:T(8,128)S(1)} %reshape.92), kind=kOutput, calls=%fused_computation.3 | convolution fusion | flops 151191168 | bytes 2135552 | tf_op jit(solution)/shard_map/ijk,kr->ijr/dot_general | solution.py:37
  34.4 0.1 copy.23
  34.5 0.1 pad_maximum_fusion
  34.5 0.1 copy.24
  34.6 0.1 broadcast_in_dim.17
  34.8 13.2 %all_to_all.22 = f32[16,1,1536]{2,1,0:T(1,128)S(1)} all-to-all(f32[16,1,1536]{2,1,0:T(1,128)S(1)} %broadcast_in_dim.18), channel_id=1, replica_groups=mesh['ia'=32,'ja'=4,'ka'=4] {'ja','ka'}, dimensions={0} | all-to-all | bytes 196608 | tf_op jit(solution)/shard_map/all_to_all | solution.py:22
  48.1 0.1 fusion.9
  48.2 0.1 mul.43
  48.3 2.2 %cholesky.16 = f32[24,24]{1,0:T(8,128)S(1)} custom-call(f32[24,24]{1,0:T(8,128)S(1)} %fusion.8), custom_call_target="Cholesky" | custom-call | tf_op jit(solution)/shard_map/jit(cholesky)/cholesky | solution.py:16
  50.6 0.6 compare_reduce_fusion
  51.2 0.6 fusion.3
  51.9 1.8 %custom-call.10 = f32[1,24,24]{1,2,0:T(8,128)S(1)} custom-call(f32[1,24,24]{2,1,0:T(8,128)S(1)} %fusion.3), custom_call_target="InvertDiagBlocksLowerTriangular" | custom-call | tf_op jit(solution)/shard_map/jit(_cho_solve)/triangular_solve | solution.py:17
  53.7 0.1 slice.67
  53.8 0.1 fusion.6
  53.9 0.1 fusion.4
  54.1 0.2 fusion.12
  54.3 0.1 broadcast_in_dim.32
  54.4 0.7 broadcast_in_dim.33
  55.1 6.4 %all-to-all-start.2 = ((f32[32,1,576]{2,1,0:T(1,128)}), f32[32,1,576]{2,1,0:T(1,128)S(1)}, u32[]{:S(2)}, u32[]{:S(2)}) async-start(f32[32,1,576]{2,1,0:T(1,128)} %broadcast_in_dim.33), calls=%async_computation.2 | async-start | bytes 163840 | tf_op jit(solution)/shard_map/all_to_all | solution.py:22
  61.5 13.8 %all-to-all-done.2 = f32[32,1,576]{2,1,0:T(1,128)S(1)} async-done(((f32[32,1,576]{2,1,0:T(1,128)}), f32[32,1,576]{2,1,0:T(1,128)S(1)}, u32[]{:S(2)}, u32[]{:S(2)}) %all-to-all-start.2) | async-done | bytes 73760 | tf_op jit(solution)/shard_map/all_to_all | solution.py:22
  75.3 0.1 reshape.93
  75.4 0.8 %gather_fusion = f32[24]{0:T(128)S(1)} fusion(f32[24,24]{1,0:T(8,128)S(1)} %reshape.93, s32[24]{0:T(128)S(1)} %or_bitcast_fusion), kind=kCustom, calls=%fused_computation | custom fusion | bytes 384 | tf_op jit(solution)/shard_map/jit(diagonal)/cond/branch_0_fun/gather | solution.py:52
  76.2 0.7 divide_multiply_fusion
  76.9 0.6 divide_bitcast_fusion
  (18 shorter events, 0.5 us)
Async XLA Ops:
  0.6 31.8 %copy-start = (f32[16,256,128]{2,1,0:T(8,128)S(1)}, f32[16,256,128]{2,1,0:T(8,128)}, u32[]{:S(2)}) copy-start(f32[16,256,128]{2,1,0:T(8,128)} %param.3) | copy-start | bytes 6291460
  55.1 20.2 %all-to-all-start.2 = ((f32[32,1,576]{2,1,0:T(1,128)}), f32[32,1,576]{2,1,0:T(1,128)S(1)}, u32[]{:S(2)}, u32[]{:S(2)}) async-start(f32[32,1,576]{2,1,0:T(1,128)} %broadcast_in_dim.33), calls=%async_computation.2 | async-start | bytes 163840 | tf_op jit(solution)/shard_map/all_to_all | solution.py:22
  76.2 1.3 %copy-start.1 = (f32[24]{0:T(128)}, f32[24]{0:T(128)S(1)}, u32[]{:S(2)}) copy-start(f32[24]{0:T(128)S(1)} %add_sqrt_fusion) | copy-start | bytes 292

commit v2 on v0

v2 whole, which is shorter than its diff:
```python
import functools

import jax
import jax.numpy as jnp
from jax import lax
from jax.experimental import pallas as pl
from jax.experimental.pallas import tpu as pltpu
from jax.sharding import Mesh, PartitionSpec as P

EPSILON = 1e-06
LANES = 128
SUBLANES = 8
BLOCK = 12


def exchange(copies, axes):
    return lax.all_to_all(copies, axes, 0, 0, tiled=True)


def lane_start(slot, rank):
    per_tile = LANES // rank
    return LANES * (slot // per_tile) + rank * (slot % per_tile)


def call(kernel, out_shape, scratch, *operands):
    vmem = pl.BlockSpec(memory_space=pltpu.VMEM)
    return pl.pallas_call(
        kernel,
        out_shape=out_shape,
        in_specs=[vmem] * len(operands),
        out_specs=jax.tree.map(lambda _: vmem, out_shape),
        scratch_shapes=scratch,
    )(*operands)


def pack_kernel(two_ref, three_ref, out_ref):
    rank = two_ref.shape[-1]
    rows = [two_ref[0, r : r + 1, :] for r in range(two_ref.shape[1])]
    rows += [three_ref[0, r : r + 1, :] for r in range(three_ref.shape[1])]
    pieces, at = [], 0
    for slot, row in enumerate(rows):
        start = lane_start(slot, rank)
        if start > at:
            pieces.append(jnp.zeros((1, start - at), jnp.float32))
        pieces.append(row)
        at = start + rank
    pieces.append(jnp.zeros((1, out_ref.shape[-1] - at), jnp.float32))
    out_ref[...] = jnp.broadcast_to(jnp.concatenate(pieces, axis=1), out_ref.shape)


def parts_of(thrice, rank):
    high = thrice.astype(jnp.bfloat16).astype(jnp.float32)
    rest = thrice - high
    middle = rest.astype(jnp.bfloat16).astype(jnp.float32)
    lane = lax.broadcasted_iota(jnp.int32, thrice.shape, 1)
    return jnp.where(
        lane < rank, high, jnp.where(lane < 2 * rank, middle, rest - middle)
    ).astype(jnp.bfloat16)


def fold_lanes(wide, rank):
    return wide[:, :rank] + wide[:, rank : 2 * rank] + wide[:, 2 * rank : 3 * rank]


def fold_gram(full, rank):
    return fold_lanes(full[:rank] + full[rank : 2 * rank] + full[2 * rank : 3 * rank], rank)


def gram_of_parts(parts, rank):
    full = lax.dot_general(
        parts, parts, (((0,), (0,)), ((), ())), preferred_element_type=jnp.float32
    )
    return fold_gram(full, rank)


def contract_kernel(
    gathered_ref, tensor_ref, out_ref, two_ref, three_ref, sums_ref, gram_two_ref, gram_three_ref,
    *, rank, cores, chips
):
    count_two = two_ref.shape[0] // (cores * chips)
    count_three = three_ref.shape[0] // (cores * chips)
    for core in range(cores):
        block = gathered_ref[core * chips : (core + 1) * chips, :]
        for slot in range(count_two + count_three):
            start = lane_start(slot, rank)
            piece = block[:, start : start + rank]
            thrice = jnp.concatenate([piece, piece, piece], axis=1)
            if slot < count_two:
                two_ref[pl.ds(count_two * core + slot, chips, stride=count_two * cores), :] = thrice
            else:
                first = count_three * core + slot - count_two
                three_ref[pl.ds(first, chips, stride=count_three * cores), :] = thrice
    two = two_ref[...]
    parts_three = parts_of(three_ref[...], rank)
    double = jnp.concatenate([parts_three, parts_three], axis=0)
    for row in range(tensor_ref.shape[0]):
        cells = tensor_ref[row]
        high = cells.astype(jnp.bfloat16)
        rest = cells - high.astype(jnp.float32)
        middle = rest.astype(jnp.bfloat16)
        low = (rest - middle.astype(jnp.float32)).astype(jnp.bfloat16)
        through = jnp.dot(
            jnp.concatenate([high, middle], axis=1), double, preferred_element_type=jnp.float32
        )
        through += jnp.dot(low, parts_three, preferred_element_type=jnp.float32)
        sums_ref[row : row + 1, :] = jnp.sum(through * two, axis=0, keepdims=True)
    partial = fold_lanes(sums_ref[...], rank).T
    gram_two_ref[...] = gram_of_parts(parts_of(two, rank), rank)
    gram_three_ref[...] = gram_of_parts(parts_three, rank)
    tiles = rank // SUBLANES
    tile_two = SUBLANES * jnp.minimum(lax.axis_index("ka"), tiles - 1)
    tile_three = SUBLANES * jnp.minimum(lax.axis_index("ja"), tiles - 1)
    pieces = [partial[SUBLANES * t : SUBLANES * (t + 1)] for t in range(tiles)]
    pieces.append(gram_two_ref[pl.ds(pl.multiple_of(tile_two, SUBLANES), SUBLANES), :])
    pieces.append(gram_three_ref[pl.ds(pl.multiple_of(tile_three, SUBLANES), SUBLANES), :])
    out_ref[...] = jnp.broadcast_to(jnp.concatenate(pieces, axis=1)[None], out_ref.shape)


def across_sublanes(tile, sublane):
    return jnp.broadcast_to(tile[sublane : sublane + 1, :], tile.shape)


def across_lanes(tile, lane):
    return jnp.broadcast_to(tile[:, lane : lane + 1], tile.shape)


def eliminate(tiles, rank):
    sublane = lax.broadcasted_iota(jnp.int32, tiles[0].shape, 0)

    def reduced(values, column, pivot_row, pivot_tile, pivot_sublane):
        out = [v - c * pivot_row for v, c in zip(values, column)]
        out[pivot_tile] = jnp.where(sublane == pivot_sublane, pivot_row, out[pivot_tile])
        return out

    for begin in range(0, rank, BLOCK):
        columns = [[across_lanes(v, begin + m) for v in tiles] for m in range(BLOCK)]
        for m in range(BLOCK):
            t, s = divmod(begin + m, SUBLANES)
            column = columns[m]
            inverse = 1.0 / across_sublanes(column[t], s)
            pivot_row = across_sublanes(tiles[t], s) * inverse
            tiles = reduced(tiles, column, pivot_row, t, s)
            for later in range(m + 1, BLOCK):
                entry = across_sublanes(columns[later][t], s) * inverse
                columns[later] = reduced(columns[later], column, entry, t, s)
    return tiles


def solve_kernel(parts_ref, out_ref, updated_ref, *, rank, rows, cores, groups_two, groups_three):
    tiles = rank // SUBLANES
    group = groups_two * groups_three
    products = []
    for core in range(cores):
        total = parts_ref[core * group]
        for source in range(1, group):
            total += parts_ref[core * group + source]
        products.append(total)
    at_two, at_three = tiles * rows, tiles * rows + rank
    augmented = []
    for t in range(tiles):
        gram_two = parts_ref[t]
        for j in range(1, groups_two):
            gram_two += parts_ref[j * groups_three + t]
        gram_three = parts_ref[t * groups_three]
        for k in range(1, groups_three):
            gram_three += parts_ref[t * groups_three + k]
        system = gram_two[:, at_two : at_two + rank] * gram_three[:, at_three : at_three + rank]
        sides = [product[:, rows * t : rows * (t + 1)] for product in products]
        augmented.append(jnp.concatenate([system] + sides, axis=1))
    solved = jnp.concatenate([v[:, rank:] for v in eliminate(augmented, rank)], axis=0)
    updated_ref[...] = solved
    high = solved.astype(jnp.bfloat16)
    rest = solved - high.astype(jnp.float32)
    middle = rest.astype(jnp.bfloat16)
    low = (rest - middle.astype(jnp.float32)).astype(jnp.bfloat16)
    stacked = jnp.concatenate([high, middle, low], axis=0)
    full = lax.dot_general(
        stacked, stacked, (((1,), (1,)), ((), ())), preferred_element_type=jnp.float32
    )
    gram = fold_gram(full, rank)
    pieces = [gram[SUBLANES * t : SUBLANES * (t + 1)] for t in range(tiles)]
    out_ref[...] = jnp.broadcast_to(jnp.concatenate(pieces, axis=1)[None], out_ref.shape)


def scale_kernel(grams_ref, updated_ref, factor_ref, rms_ref, correlation_ref, *, rank, total_rows):
    total = grams_ref[0]
    for source in range(1, grams_ref.shape[0]):
        total += grams_ref[source]
    gram = jnp.concatenate(
        [total[:, rank * t : rank * (t + 1)] for t in range(rank // SUBLANES)], axis=0
    )
    diagonal = jnp.where(
        lax.broadcasted_iota(jnp.int32, gram.shape, 0) == lax.broadcasted_iota(jnp.int32, gram.shape, 1),
        gram,
        0.0,
    )
    rms_row = jnp.sqrt(jnp.sum(diagonal, axis=0, keepdims=True) / total_rows + EPSILON)
    rms_column = jnp.sqrt(jnp.sum(diagonal, axis=1, keepdims=True) / total_rows + EPSILON)
    rms_ref[...] = rms_row
    factor_ref[...] = updated_ref[...] / rms_row
    correlation_ref[...] = gram / (rms_column * rms_row) / total_rows


def per_device(tensor, second_factor, third_factor):
    f32 = jnp.float32
    rank = second_factor.shape[-1]
    chips, cores = lax.axis_size("z"), lax.axis_size("core")
    groups_two, groups_three = lax.axis_size("ja"), lax.axis_size("ka")
    members = chips * cores
    rows = tensor.shape[0]
    total_rows = rows * members
    slots = second_factor.shape[1] + third_factor.shape[1]
    width = -(-(lane_start(slots - 1, rank) + rank) // LANES) * LANES
    tiles = rank // SUBLANES

    packed = call(
        pack_kernel, jax.ShapeDtypeStruct((members, width), f32), [], second_factor, third_factor
    )
    gathered = exchange(packed, ("core", "z"))

    messages = call(
        functools.partial(contract_kernel, rank=rank, cores=cores, chips=chips),
        jax.ShapeDtypeStruct((cores * groups_two * groups_three, SUBLANES, tiles * rows + 2 * rank), f32),
        [
            pltpu.VMEM((tensor.shape[1], 3 * rank), f32),
            pltpu.VMEM((tensor.shape[2], 3 * rank), f32),
            pltpu.VMEM((rows, 3 * rank), f32),
            pltpu.VMEM((rank, rank), f32),
            pltpu.VMEM((rank, rank), f32),
        ],
        gathered,
        tensor,
    )
    parts = exchange(messages, ("core", "ja", "ka"))

    grams, solved = call(
        functools.partial(
            solve_kernel, rank=rank, rows=rows, cores=cores, groups_two=groups_two, groups_three=groups_three
        ),
        (
            jax.ShapeDtypeStruct((chips, SUBLANES, tiles * rank), f32),
            jax.ShapeDtypeStruct((rank, cores * rows), f32),
        ),
        [],
        parts,
    )
    grams = exchange(grams, "z")
    updated = lax.dynamic_slice_in_dim(solved.T, lax.axis_index("core") * rows, rows, 0)

    factor, column_rms, correlation = call(
        functools.partial(scale_kernel, rank=rank, total_rows=total_rows),
        (
            jax.ShapeDtypeStruct((rows, rank), f32),
            jax.ShapeDtypeStruct((1, rank), f32),
            jax.ShapeDtypeStruct((rank, rank), f32),
        ),
        [],
        grams,
        updated,
    )
    return (factor, column_rms[0], correlation)


def solution(mesh):
    ia, ja, ka = (mesh.shape[name] for name in ("ia", "ja", "ka"))
    split = Mesh(mesh.devices.reshape(ia // 2, 2, ja, ka), ("z", "core", "ja", "ka"))
    first = ("z", "core")
    return jax.shard_map(
        per_device,
        mesh=split,
        in_specs=(P(first, "ja", "ka"), P("ja", first, None), P("ka", first, None)),
        out_specs=(P(first, None), P(), P()),
        check_vma=False,
    )
```

time: 236 us -> 72.1 us (0.31)
  blocking collectives: 222 us -> 44.5 us
  waiting for transfers between devices: 0 us -> 10.2 us
  Pallas kernels: 0 us -> 9.26 us
  other arithmetic: 6.67 us -> 0 us
  matrix products: 5.09 us -> 0 us
  starting transfers between devices: 0 us -> 3.49 us
  local copies, waits for them, and re-layouts: 0.92 us -> 3.47 us
    psum x4 -> x0, blocking collectives: 152 us -> none  [the longest x1 97.1 us: per_device(): gram_first = lax.psum(gram_of(updated), 'ia')]
    all_gather x2 -> x0, blocking collectives: 69.3 us -> none  [the longest x1 38.1 us: per_device(): lax.all_gather(third_factor, 'ia', axis=1, tiled=True)]
    all_to_all x0 -> x2, blocking collectives: none -> 44.5 us  [exchange(): return lax.all_to_all(copies, axes, 0, 0, tiled=True)]
    all_to_all x0 -> x1, waiting for transfers between devices: none -> 10.2 us  [exchange(): return lax.all_to_all(copies, axes, 0, 0, tiled=True)]
    pallas_call x0 -> x4, Pallas kernels: none -> 9.26 us  [call(): pl.pallas_call(kernel, out_shape=out_shape, in_specs=[vmem] * len(operand...]
    another operation x5 -> x0, other arithmetic: 5.34 us -> none  [the longest x3 2.86 us: solve_rows(): lower_factor = jnp.linalg.cholesky(system)]
    dot_general x4 -> x0, matrix products: 4.8 us -> none  [the longest x1 4.01 us: per_device(): lax.dot_general(flattened, paired, (((1,), (1,)), ((), ())), precision=hi...]
    all_to_all x0 -> x1, starting transfers between devices: none -> 3.49 us  [exchange(): return lax.all_to_all(copies, axes, 0, 0, tiled=True)]
  transfers between devices with their start and end apart: 0 -> 1, of which waited for: 0 -> 1; matrix products, arithmetic and copies ran while one was open for 0% -> 2% of each run, Pallas kernels for 0% -> 0%
where the time goes in v2:
time: 72.1 us; the launch traced here: 71.6 us
  blocking collectives  44.5 us (62%)
  waiting for transfers between devices  10.2 us (14%)
  Pallas kernels  9.26 us (13%)
  starting transfers between devices  3.49 us (5%)
  local copies, waits for them, and re-layouts  3.47 us (5%)
    all_to_all x2, blocking collectives, exchange(): return lax.all_to_all(copies, axes, 0, 0, tiled=True)  44.5 us
    all_to_all x1, waiting for transfers between devices, exchange(): return lax.all_to_all(copies, axes, 0, 0, tiled=True)  10.2 us
    pallas_call x4, Pallas kernels, call(): pl.pallas_call(kernel, out_shape=out_shape, in_specs=[vmem] * len(operand...  9.26 us
    all_to_all x1, starting transfers between devices, exchange(): return lax.all_to_all(copies, axes, 0, 0, tiled=True)  3.49 us
  transfers between devices with their start and end apart: 1, of which 1 were waited for; matrix products, arithmetic and copies ran while one was open for 2% of the time, Pallas kernels for 0%

profile of v2, /device:TPU:1, one launch (start us, length us, event | category | flops | bytes accessed | tf_op | source)
XLA Modules:
  0.0 71.6 jit_solution(12584323103459189793)
XLA Ops:
  0.6 1.4 %shard_map.58 = f32[32,384]{1,0:T(8,128)} custom-call(f32[1,8,24]{2,1,0:T(8,128)} %two_ref.1, f32[1,4,24]{2,1,0:T(4,128)} %three_ref.1), custom_call_target="tpu_custom_call" | custom-call | tf_op jit(solution)/shard_map/pallas_call | solution.py:27
  2.0 0.8 %copy.7 = f32[32,1,384]{2,1,0:T(1,128)S(1)} copy(f32[32,1,384]{2,0,1:T(8,128)} %bitcast.7) | data formatting | bytes 98304 | tf_op jit(solution)/shard_map/all_to_all | solution.py:17
  2.9 29.7 %all_to_all.21 = f32[32,1,384]{2,1,0:T(1,128)S(1)} all-to-all(f32[32,1,384]{2,1,0:T(1,128)S(1)} %copy.7), channel_id=1, replica_groups=mesh['z'=16,'core'=2,'ja'=4,'ka'=4] {'core','z'}, dimensions={0} | all-to-all | bytes 98304 | tf_op jit(solution)/shard_map/all_to_all | solution.py:17
  32.5 0.6 copy.11
  33.1 3.6 %shard_map.59 = f32[32,8,96]{2,1,0:T(8,128)} custom-call(f32[32,384]{1,0:T(8,128)} %bitcast.8, f32[16,256,128]{2,1,0:T(8,128)} %tensor_ref.1), custom_call_target="tpu_custom_call" | custom-call | tf_op jit(solution)/shard_map/pallas_call | solution.py:27
  36.8 14.8 %all_to_all.22.parts_ref = f32[32,8,96]{2,1,0:T(8,128)} all-to-all(f32[32,8,96]{2,1,0:T(8,128)} %shard_map.59), channel_id=1, replica_groups=mesh['z'=16,'core'=2,'ja'=4,'ka'=4] {'core','ja','ka'}, dimensions={0} | all-to-all | bytes 196608 | tf_op jit(solution)/shard_map/all_to_all | solution.py:17
  51.6 2.6 %shard_map.60 = (f32[16,8,72]{2,1,0:T(8,128)}, f32[24,32]{1,0:T(8,128)}) custom-call(f32[32,8,96]{2,1,0:T(8,128)} %all_to_all.22.parts_ref), custom_call_target="tpu_custom_call" | custom-call | tf_op jit(solution)/shard_map/pallas_call | solution.py:27
  54.2 3.5 %all-to-all-start.2 = ((f32[16,8,72]{2,1,0:T(8,128)}), f32[16,8,72]{2,1,0:T(8,128)S(1)}, u32[]{:S(2)}, u32[]{:S(2)}) async-start(f32[16,8,72]{2,1,0:T(8,128)} %get-tuple-element.8), calls=%async_computation.2 | async-start | bytes 131072 | tf_op jit(solution)/shard_map/all_to_all | solution.py:17
  57.7 0.8 %copy.8 = f32[24,32]{0,1:T(8,128)S(1)} copy(f32[24,32]{1,0:T(8,128)} %get-tuple-element.9) | data formatting | bytes 6144 | tf_op jit(solution)/shard_map/pallas_call | solution.py:27
  58.5 0.6 dynamic-slice_bitcast_fusion.updated_ref
  59.1 10.2 %all-to-all-done.2.grams_ref = f32[16,8,72]{2,1,0:T(8,128)S(1)} async-done(((f32[16,8,72]{2,1,0:T(8,128)}), f32[16,8,72]{2,1,0:T(8,128)S(1)}, u32[]{:S(2)}, u32[]{:S(2)}) %all-to-all-start.2) | async-done | bytes 36896 | tf_op jit(solution)/shard_map/all_to_all | solution.py:17
  69.4 0.0 copy-start
  69.4 0.6 copy-done
  70.0 1.6 %shard_map.61 = (f32[16,24]{1,0:T(8,128)}, f32[1,24]{1,0:T(1,128)}, f32[24,24]{1,0:T(8,128)}) custom-call(f32[16,8,72]{2,1,0:T(8,128)} %copy-done, f32[16,24]{1,0:T(8,128)} %dynamic-slice_bitcast_fusion.updated_ref), custom_call_target="tpu_custom_call" | custom-call | tf_op jit(solution)/shard_map/pallas_call | solution.py:27
Async XLA Ops:
  54.2 15.1 %all-to-all-start.2 = ((f32[16,8,72]{2,1,0:T(8,128)}), f32[16,8,72]{2,1,0:T(8,128)S(1)}, u32[]{:S(2)}, u32[]{:S(2)}) async-start(f32[16,8,72]{2,1,0:T(8,128)} %get-tuple-element.8), calls=%async_computation.2 | async-start | bytes 131072 | tf_op jit(solution)/shard_map/all_to_all | solution.py:17
  69.4 0.6 copy-start

commit v3 on v2

--- a/solution.py
+++ b/solution.py
@@ -11,6 +11,7 @@
 LANES = 128
 SUBLANES = 8
 BLOCK = 12
+VMEM_BYTES = 8 * 2**20
 
 
 def exchange(copies, axes):
@@ -22,18 +23,28 @@
     return LANES * (slot // per_tile) + rank * (slot % per_tile)
 
 
-def call(kernel, out_shape, scratch, *operands):
-    vmem = pl.BlockSpec(memory_space=pltpu.VMEM)
+def call(kernel, out_shape, scratch, *operands, fetched=(), cost=None):
+    vmem, hbm = pl.BlockSpec(memory_space=pltpu.VMEM), pl.BlockSpec(memory_space=pltpu.HBM)
     return pl.pallas_call(
         kernel,
         out_shape=out_shape,
-        in_specs=[vmem] * len(operands),
+        in_specs=[hbm if at in fetched else vmem for at in range(len(operands))],
         out_specs=jax.tree.map(lambda _: vmem, out_shape),
         scratch_shapes=scratch,
+        cost_estimate=cost,
+        compiler_params=pltpu.CompilerParams(vmem_limit_bytes=VMEM_BYTES),
     )(*operands)
 
 
-def pack_kernel(two_ref, three_ref, out_ref):
+def pack_kernel(two_hbm, three_hbm, out_ref, two_ref, three_ref, arrived):
+    copies = [
+        pltpu.make_async_copy(two_hbm, two_ref, arrived.at[0]),
+        pltpu.make_async_copy(three_hbm, three_ref, arrived.at[1]),
+    ]
+    for copy in copies:
+        copy.start()
+    for copy in copies:
+        copy.wait()
     rank = two_ref.shape[-1]
     rows = [two_ref[0, r : r + 1, :] for r in range(two_ref.shape[1])]
     rows += [three_ref[0, r : r + 1, :] for r in range(three_ref.shape[1])]
@@ -45,7 +56,7 @@
         pieces.append(row)
         at = start + rank
     pieces.append(jnp.zeros((1, out_ref.shape[-1] - at), jnp.float32))
-    out_ref[...] = jnp.broadcast_to(jnp.concatenate(pieces, axis=1), out_ref.shape)
+    out_ref[...] = jnp.broadcast_to(jnp.concatenate(pieces, axis=1)[None], out_ref.shape)
 
 
 def parts_of(thrice, rank):
@@ -73,9 +84,23 @@
     return fold_gram(full, rank)
 
 
+def split_kernel(tensor_ref, upper_ref, low_ref):
+    width = tensor_ref.shape[-1]
+
+    @pl.loop(0, tensor_ref.shape[0])
+    def _(row):
+        cells = tensor_ref[row]
+        high = cells.astype(jnp.bfloat16)
+        rest = cells - high.astype(jnp.float32)
+        middle = rest.astype(jnp.bfloat16)
+        upper_ref[row, :, :width] = high
+        upper_ref[row, :, width:] = middle
+        low_ref[row] = (rest - middle.astype(jnp.float32)).astype(jnp.bfloat16)
+
+
 def contract_kernel(
-    gathered_ref, tensor_ref, out_ref, two_ref, three_ref, sums_ref, gram_two_ref, gram_three_ref,
-    *, rank, cores, chips
+    gathered_ref, upper_ref, low_ref, out_ref, two_ref, three_ref, sums_ref,
+    gram_two_ref, gram_three_ref, *, rank, cores, chips
 ):
     count_two = two_ref.shape[0] // (cores * chips)
     count_three = three_ref.shape[0] // (cores * chips)
@@ -93,16 +118,9 @@
     two = two_ref[...]
     parts_three = parts_of(three_ref[...], rank)
     double = jnp.concatenate([parts_three, parts_three], axis=0)
-    for row in range(tensor_ref.shape[0]):
-        cells = tensor_ref[row]
-        high = cells.astype(jnp.bfloat16)
-        rest = cells - high.astype(jnp.float32)
-        middle = rest.astype(jnp.bfloat16)
-        low = (rest - middle.astype(jnp.float32)).astype(jnp.bfloat16)
-        through = jnp.dot(
-            jnp.concatenate([high, middle], axis=1), double, preferred_element_type=jnp.float32
-        )
-        through += jnp.dot(low, parts_three, preferred_element_type=jnp.float32)
+    for row in range(upper_ref.shape[0]):
+        through = jnp.dot(upper_ref[row], double, preferred_element_type=jnp.float32)
+        through += jnp.dot(low_ref[row], parts_three, preferred_element_type=jnp.float32)
         sums_ref[row : row + 1, :] = jnp.sum(through * two, axis=0, keepdims=True)
     partial = fold_lanes(sums_ref[...], rank).T
     gram_two_ref[...] = gram_of_parts(parts_of(two, rank), rank)
@@ -146,7 +164,7 @@
     return tiles
 
 
-def solve_kernel(parts_ref, out_ref, updated_ref, *, rank, rows, cores, groups_two, groups_three):
+def solve_kernel(parts_ref, out_ref, updated_ref, chip_ref, *, rank, rows, cores, groups_two, groups_three):
     tiles = rank // SUBLANES
     group = groups_two * groups_three
     products = []
@@ -168,7 +186,9 @@
         sides = [product[:, rows * t : rows * (t + 1)] for product in products]
         augmented.append(jnp.concatenate([system] + sides, axis=1))
     solved = jnp.concatenate([v[:, rank:] for v in eliminate(augmented, rank)], axis=0)
-    updated_ref[...] = solved
+    chip_ref[...] = solved.T
+    first = pl.multiple_of(rows * lax.axis_index("core"), SUBLANES)
+    updated_ref[...] = chip_ref[pl.ds(first, rows), :]
     high = solved.astype(jnp.bfloat16)
     rest = solved - high.astype(jnp.float32)
     middle = rest.astype(jnp.bfloat16)
@@ -203,6 +223,9 @@
 
 def per_device(tensor, second_factor, third_factor):
     f32 = jnp.float32
+    second_factor, third_factor = (
+        pltpu.with_memory_space_constraint(v, pltpu.HBM) for v in (second_factor, third_factor)
+    )
     rank = second_factor.shape[-1]
     chips, cores = lax.axis_size("z"), lax.axis_size("core")
     groups_two, groups_three = lax.axis_size("ja"), lax.axis_size("ka")
@@ -214,10 +237,29 @@
     tiles = rank // SUBLANES
 
     packed = call(
-        pack_kernel, jax.ShapeDtypeStruct((members, width), f32), [], second_factor, third_factor
-    )
-    gathered = exchange(packed, ("core", "z"))
-
+        pack_kernel,
+        jax.ShapeDtypeStruct((members, 1, width), f32),
+        [
+            pltpu.VMEM(second_factor.shape, f32),
+            pltpu.VMEM(third_factor.shape, f32),
+            pltpu.SemaphoreType.DMA((2,)),
+        ],
+        second_factor,
+        third_factor,
+        fetched=(0, 1),
+    )
+    gathered = exchange(packed, ("core", "z")).reshape(members, width)
+
+    upper, low = call(
+        split_kernel,
+        (
+            jax.ShapeDtypeStruct((*tensor.shape[:2], 2 * tensor.shape[2]), jnp.bfloat16),
+            jax.ShapeDtypeStruct(tensor.shape, jnp.bfloat16),
+        ),
+        [],
+        tensor,
+        cost=pl.CostEstimate(flops=5 * tensor.size, bytes_accessed=10 * tensor.size, transcendentals=0),
+    )
     messages = call(
         functools.partial(contract_kernel, rank=rank, cores=cores, chips=chips),
         jax.ShapeDtypeStruct((cores * groups_two * groups_three, SUBLANES, tiles * rows + 2 * rank), f32),
@@ -229,23 +271,23 @@
             pltpu.VMEM((rank, rank), f32),
         ],
         gathered,
-        tensor,
+        upper,
+        low,
     )
     parts = exchange(messages, ("core", "ja", "ka"))
 
-    grams, solved = call(
+    grams, updated = call(
         functools.partial(
             solve_kernel, rank=rank, rows=rows, cores=cores, groups_two=groups_two, groups_three=groups_three
         ),
         (
             jax.ShapeDtypeStruct((chips, SUBLANES, tiles * rank), f32),
-            jax.ShapeDtypeStruct((rank, cores * rows), f32),
+            jax.ShapeDtypeStruct((rows, rank), f32),
         ),
-        [],
+        [pltpu.VMEM((cores * rows, rank), f32)],
         parts,
     )
     grams = exchange(grams, "z")
-    updated = lax.dynamic_slice_in_dim(solved.T, lax.axis_index("core") * rows, rows, 0)
 
     factor, column_rms, correlation = call(
         functools.partial(scale_kernel, rank=rank, total_rows=total_rows),

time: 72.1 us -> 64.2 us (0.89)
  blocking collectives: 44.5 us -> 28.8 us
  starting transfers between devices: 3.49 us -> 16.8 us
  Pallas kernels: 9.26 us -> 5.23 us
  local copies, waits for them, and re-layouts: 3.47 us -> 1.59 us
    all_to_all x2, blocking collectives: 44.5 us -> 28.8 us  [exchange(): return lax.all_to_all(copies, axes, 0, 0, tiled=True)]
    all_to_all x1, starting transfers between devices: 3.49 us -> 16.8 us  [exchange(): return lax.all_to_all(copies, axes, 0, 0, tiled=True)]
    pallas_call x4 -> x5, Pallas kernels: 9.26 us -> 5.23 us  [call(): pl.pallas_call(kernel, out_shape=out_shape, in_specs=[hbm if at in fetche...]
    all_to_all x1 -> x0, local copies, waits for them, and re-layouts: 0.85 us -> none  [exchange(): return lax.all_to_all(copies, axes, 0, 0, tiled=True)]
    pallas_call x1 -> x0, local copies, waits for them, and re-layouts: 0.78 us -> none  [call(): pl.pallas_call(kernel, out_shape=out_shape, in_specs=[vmem] * len(operand...]
  transfers between devices with their start and end apart: 1 -> 1, of which waited for: 1 -> 1; matrix products, arithmetic and copies ran while one was open for 2% -> 0% of each run, Pallas kernels for 0% -> 1%
where the time goes in v3:
time: 64.2 us; the launch traced here: 63.9 us
  blocking collectives  28.8 us (45%)
  starting transfers between devices  16.8 us (26%)
  waiting for transfers between devices  10.9 us (17%)
  Pallas kernels  5.23 us (8%)
  local copies, waits for them, and re-layouts  1.59 us (2%)
  between operations  0.68 us (1%)
    all_to_all x2, blocking collectives, exchange(): return lax.all_to_all(copies, axes, 0, 0, tiled=True)  28.8 us
    all_to_all x1, starting transfers between devices, exchange(): return lax.all_to_all(copies, axes, 0, 0, tiled=True)  16.8 us
    all_to_all x1, waiting for transfers between devices, exchange(): return lax.all_to_all(copies, axes, 0, 0, tiled=True)  10.9 us
    pallas_call x5, Pallas kernels, call(): pl.pallas_call(kernel, out_shape=out_shape, in_specs=[hbm if at in fetche...  5.23 us
    unnamed x3, local copies, waits for them, and re-layouts  1.59 us
  transfers between devices with their start and end apart: 1, of which 1 were waited for; matrix products, arithmetic and copies ran while one was open for 0% of the time, Pallas kernels for 1%

profile of v3, /device:TPU:1, one launch (start us, length us, event | category | flops | bytes accessed | tf_op | source)
XLA Modules:
  0.0 63.9 jit_solution(2861487574135357773)
XLA Ops:
  0.6 1.4 %shard_map.58 = f32[32,1,384]{2,1,0:T(1,128)} custom-call(f32[1,8,24]{2,1,0:T(8,128)} %two_hbm.1, f32[1,4,24]{2,1,0:T(4,128)} %three_hbm.1), custom_call_target="tpu_custom_call" | custom-call | tf_op jit(solution)/shard_map/pallas_call | solution.py:28
  2.1 16.8 %all-to-all-start = ((f32[32,1,384]{2,1,0:T(1,128)}), f32[32,1,384]{2,1,0:T(1,128)S(1)}, u32[]{:S(2)}, u32[]{:S(2)}) async-start(f32[32,1,384]{2,1,0:T(1,128)} %shard_map.58), calls=%async_computation | async-start | bytes 98304 | tf_op jit(solution)/shard_map/all_to_all | solution.py:18
  18.8 0.0 copy-start
  18.8 1.6 %copy-done = f32[16,256,128]{2,1,0:T(8,128)S(1)} copy-done((f32[16,256,128]{2,1,0:T(8,128)S(1)}, f32[16,256,128]{2,1,0:T(8,128)}, u32[]{:S(2)}) %copy-start) | copy-done | bytes 2097176
  20.4 0.6 shard_map.59
  21.0 10.9 %all-to-all-done = f32[32,1,384]{2,1,0:T(1,128)S(1)} async-done(((f32[32,1,384]{2,1,0:T(1,128)}), f32[32,1,384]{2,1,0:T(1,128)S(1)}, u32[]{:S(2)}, u32[]{:S(2)}) %all-to-all-start) | async-done | bytes 49184 | tf_op jit(solution)/shard_map/all_to_all | solution.py:18
  31.9 1.3 %shard_map.60 = f32[32,8,96]{2,1,0:T(8,128)S(1)} custom-call(f32[32,384]{1,0:T(8,128)S(1)} %bitcast.4, bf16[16,256,256]{2,1,0:T(8,128)(2,1)S(1)} %get-tuple-element.10.upper_ref, bf16[16,256,128]{2,1,0:T(8,128)(2,1)S(1)} %get-tuple-element.11.low_ref), custom_call_target="tpu_custom_call" | custom-call | tf_op jit(solution)/shard_map/pallas_call | solution.py:28
  33.3 14.5 %all_to_all.15.parts_ref = f32[32,8,96]{2,1,0:T(8,128)S(1)} all-to-all(f32[32,8,96]{2,1,0:T(8,128)S(1)} %shard_map.60), channel_id=1, replica_groups=mesh['z'=16,'core'=2,'ja'=4,'ka'=4] {'core','ja','ka'}, dimensions={0} | all-to-all | bytes 196608 | tf_op jit(solution)/shard_map/all_to_all | solution.py:18
  47.8 1.1 %shard_map.61 = (f32[16,8,72]{2,1,0:T(8,128)S(1)}, f32[16,24]{1,0:T(8,128)S(1)}) custom-call(f32[32,8,96]{2,1,0:T(8,128)S(1)} %all_to_all.15.parts_ref), custom_call_target="tpu_custom_call" | custom-call | tf_op jit(solution)/shard_map/pallas_call | solution.py:28
  48.9 14.2 %all_to_all.16.grams_ref = f32[16,8,72]{2,1,0:T(8,128)S(1)} all-to-all(f32[16,8,72]{2,1,0:T(8,128)S(1)} %get-tuple-element.12), channel_id=1, replica_groups=mesh['z'=16,'core'=2,'ja'=4,'ka'=4] {'z'}, dimensions={0} | all-to-all | bytes 73728 | tf_op jit(solution)/shard_map/all_to_all | solution.py:18
  63.2 0.8 %shard_map.62 = (f32[16,24]{1,0:T(8,128)}, f32[1,24]{1,0:T(1,128)}, f32[24,24]{1,0:T(8,128)}) custom-call(f32[16,8,72]{2,1,0:T(8,128)S(1)} %all_to_all.16.grams_ref, f32[16,24]{1,0:T(8,128)S(1)} %get-tuple-element.13.updated_ref), custom_call_target="tpu_custom_call" | custom-call | tf_op jit(solution)/shard_map/pallas_call | solution.py:28
  (1 shorter events, 0.0 us)
Async XLA Ops:
  2.1 29.9 %all-to-all-start = ((f32[32,1,384]{2,1,0:T(1,128)}), f32[32,1,384]{2,1,0:T(1,128)S(1)}, u32[]{:S(2)}, u32[]{:S(2)}) async-start(f32[32,1,384]{2,1,0:T(1,128)} %shard_map.58), calls=%async_computation | async-start | bytes 98304 | tf_op jit(solution)/shard_map/all_to_all | solution.py:18
  18.8 1.6 %copy-start = (f32[16,256,128]{2,1,0:T(8,128)S(1)}, f32[16,256,128]{2,1,0:T(8,128)}, u32[]{:S(2)}) copy-start(f32[16,256,128]{2,1,0:T(8,128)} %tensor_ref.1) | copy-start | bytes 6291460

commit v4 on v3

--- a/solution.py
+++ b/solution.py
@@ -1,7 +1,9 @@
 import functools
+import itertools
 
 import jax
 import jax.numpy as jnp
+import numpy as np
 from jax import lax
 from jax.experimental import pallas as pl
 from jax.experimental.pallas import tpu as pltpu
@@ -14,8 +16,17 @@
 VMEM_BYTES = 8 * 2**20
 
 
-def exchange(copies, axes):
-    return lax.all_to_all(copies, axes, 0, 0, tiled=True)
+def counted_from(start, size):
+    return [(start + step) % size for step in range(size)]
+
+
+def exchange(copies, axes, starts):
+    sizes = [lax.axis_size(axis) for axis in axes]
+    order = [
+        int(np.ravel_multi_index(member, sizes))
+        for member in itertools.product(*map(counted_from, starts, sizes))
+    ]
+    return lax.all_to_all(copies, axes, 0, 0, tiled=True, axis_index_groups=[order])
 
 
 def lane_start(slot, rank):
@@ -95,33 +106,56 @@
         middle = rest.astype(jnp.bfloat16)
         upper_ref[row, :, :width] = high
         upper_ref[row, :, width:] = middle
-        low_ref[row] = (rest - middle.astype(jnp.float32)).astype(jnp.bfloat16)
+        low = (rest - middle.astype(jnp.float32)).astype(jnp.bfloat16)
+        half = tensor_ref.shape[0] // 2
+
+        @pl.when(row < half)
+        def _():
+            low_ref[row, :, :width] = low
+
+        @pl.when(row >= half)
+        def _():
+            low_ref[row - half, :, width:] = low
+
+
+def runs_from(start, size):
+    return [(0, start, size - start)] + ([(size - start, 0, start)] if start else [])
 
 
 def contract_kernel(
     gathered_ref, upper_ref, low_ref, out_ref, two_ref, three_ref, sums_ref,
-    gram_two_ref, gram_three_ref, *, rank, cores, chips
+    gram_two_ref, gram_three_ref, *, rank, cores, chips, starts
 ):
     count_two = two_ref.shape[0] // (cores * chips)
     count_three = three_ref.shape[0] // (cores * chips)
-    for core in range(cores):
-        block = gathered_ref[core * chips : (core + 1) * chips, :]
-        for slot in range(count_two + count_three):
-            start = lane_start(slot, rank)
-            piece = block[:, start : start + rank]
-            thrice = jnp.concatenate([piece, piece, piece], axis=1)
-            if slot < count_two:
-                two_ref[pl.ds(count_two * core + slot, chips, stride=count_two * cores), :] = thrice
-            else:
-                first = count_three * core + slot - count_two
-                three_ref[pl.ds(first, chips, stride=count_three * cores), :] = thrice
+    for at, core in enumerate(counted_from(starts[0], cores)):
+        for first, chip, run in runs_from(starts[1], chips):
+            block = gathered_ref[at * chips + first : at * chips + first + run, :]
+            for slot in range(count_two + count_three):
+                start = lane_start(slot, rank)
+                piece = block[:, start : start + rank]
+                thrice = jnp.concatenate([piece, piece, piece], axis=1)
+                ref, count, row = (
+                    (two_ref, count_two, slot) if slot < count_two else (three_ref, count_three, slot - count_two)
+                )
+                row += count * (cores * chip + core)
+                ref[pl.ds(row, run, stride=count * cores), :] = thrice
     two = two_ref[...]
     parts_three = parts_of(three_ref[...], rank)
     double = jnp.concatenate([parts_three, parts_three], axis=0)
-    for row in range(upper_ref.shape[0]):
-        through = jnp.dot(upper_ref[row], double, preferred_element_type=jnp.float32)
-        through += jnp.dot(low_ref[row], parts_three, preferred_element_type=jnp.float32)
-        sums_ref[row : row + 1, :] = jnp.sum(through * two, axis=0, keepdims=True)
+    blank = jnp.zeros((parts_three.shape[0], LANES - parts_three.shape[1]), jnp.bfloat16)
+    padded = jnp.concatenate([parts_three, blank], axis=1)
+    empty = jnp.zeros_like(padded)
+    diagonal = jnp.concatenate(
+        [jnp.concatenate([padded, empty], axis=1), jnp.concatenate([empty, padded], axis=1)], axis=0
+    )
+    half = low_ref.shape[0]
+    for row in range(half):
+        lows = jnp.dot(low_ref[row], diagonal, preferred_element_type=jnp.float32)
+        for each, lane in ((row, 0), (row + half, LANES)):
+            through = jnp.dot(upper_ref[each], double, preferred_element_type=jnp.float32)
+            through += lows[:, lane : lane + 3 * rank]
+            sums_ref[each : each + 1, :] = jnp.sum(through * two, axis=0, keepdims=True)
     partial = fold_lanes(sums_ref[...], rank).T
     gram_two_ref[...] = gram_of_parts(parts_of(two, rank), rank)
     gram_three_ref[...] = gram_of_parts(parts_three, rank)
@@ -164,24 +198,31 @@
     return tiles
 
 
-def solve_kernel(parts_ref, out_ref, updated_ref, chip_ref, *, rank, rows, cores, groups_two, groups_three):
+def solve_kernel(parts_ref, out_ref, updated_ref, chip_ref, *, rank, rows, cores, groups_two, groups_three, starts):
     tiles = rank // SUBLANES
     group = groups_two * groups_three
+    place = {
+        member: at
+        for at, member in enumerate(
+            itertools.product(*map(counted_from, starts, (cores, groups_two, groups_three)))
+        )
+    }
     products = []
     for core in range(cores):
-        total = parts_ref[core * group]
+        first = place[core, starts[1], starts[2]]
+        total = parts_ref[first]
         for source in range(1, group):
-            total += parts_ref[core * group + source]
+            total += parts_ref[first + source]
         products.append(total)
     at_two, at_three = tiles * rows, tiles * rows + rank
     augmented = []
     for t in range(tiles):
-        gram_two = parts_ref[t]
+        gram_two = parts_ref[place[0, 0, t]]
         for j in range(1, groups_two):
-            gram_two += parts_ref[j * groups_three + t]
-        gram_three = parts_ref[t * groups_three]
+            gram_two += parts_ref[place[0, j, t]]
+        gram_three = parts_ref[place[0, t, 0]]
         for k in range(1, groups_three):
-            gram_three += parts_ref[t * groups_three + k]
+            gram_three += parts_ref[place[0, t, k]]
         system = gram_two[:, at_two : at_two + rank] * gram_three[:, at_three : at_three + rank]
         sides = [product[:, rows * t : rows * (t + 1)] for product in products]
         augmented.append(jnp.concatenate([system] + sides, axis=1))
@@ -248,20 +289,22 @@
         third_factor,
         fetched=(0, 1),
     )
-    gathered = exchange(packed, ("core", "z")).reshape(members, width)
+    rows_from = (cores - 1, chips // 2)
+    plane_from = (cores - 1, groups_two // 2, groups_three // 2)
+    gathered = exchange(packed, ("core", "z"), rows_from).reshape(members, width)
 
     upper, low = call(
         split_kernel,
         (
             jax.ShapeDtypeStruct((*tensor.shape[:2], 2 * tensor.shape[2]), jnp.bfloat16),
-            jax.ShapeDtypeStruct(tensor.shape, jnp.bfloat16),
+            jax.ShapeDtypeStruct((rows // 2, tensor.shape[1], 2 * tensor.shape[2]), jnp.bfloat16),
         ),
         [],
         tensor,
         cost=pl.CostEstimate(flops=5 * tensor.size, bytes_accessed=10 * tensor.size, transcendentals=0),
     )
     messages = call(
-        functools.partial(contract_kernel, rank=rank, cores=cores, chips=chips),
+        functools.partial(contract_kernel, rank=rank, cores=cores, chips=chips, starts=rows_from),
         jax.ShapeDtypeStruct((cores * groups_two * groups_three, SUBLANES, tiles * rows + 2 * rank), f32),
         [
             pltpu.VMEM((tensor.shape[1], 3 * rank), f32),
@@ -274,11 +317,17 @@
         upper,
         low,
     )
-    parts = exchange(messages, ("core", "ja", "ka"))
+    parts = exchange(messages, ("core", "ja", "ka"), plane_from)
 
     grams, updated = call(
         functools.partial(
-            solve_kernel, rank=rank, rows=rows, cores=cores, groups_two=groups_two, groups_three=groups_three
+            solve_kernel,
+            rank=rank,
+            rows=rows,
+            cores=cores,
+            groups_two=groups_two,
+            groups_three=groups_three,
+            starts=plane_from,
         ),
         (
             jax.ShapeDtypeStruct((chips, SUBLANES, tiles * rank), f32),
@@ -287,7 +336,7 @@
         [pltpu.VMEM((cores * rows, rank), f32)],
         parts,
     )
-    grams = exchange(grams, "z")
+    grams = exchange(grams, ("z",), (chips // 2,))
 
     factor, column_rms, correlation = call(
         functools.partial(scale_kernel, rank=rank, total_rows=total_rows),

time: 64.2 us -> 56.3 us (0.88)
  waiting for transfers between devices: 10.9 us -> 1.17 us
  starting transfers between devices: 16.8 us -> 19.8 us
  blocking collectives: 28.8 us -> 27.3 us
    all_to_all x1, waiting for transfers between devices: 10.9 us -> 1.17 us  [exchange(): lax.all_to_all(copies, axes, 0, 0, tiled=True, axis_index_groups=[order])]
    all_to_all x1, starting transfers between devices: 16.8 us -> 19.8 us  [exchange(): lax.all_to_all(copies, axes, 0, 0, tiled=True, axis_index_groups=[order])]
    all_to_all x2, blocking collectives: 28.8 us -> 27.3 us  [exchange(): lax.all_to_all(copies, axes, 0, 0, tiled=True, axis_index_groups=[order])]
where the time goes in v4:
time: 56.3 us; the launch traced here: 56 us
  blocking collectives  27.3 us (48%)
  starting transfers between devices  19.8 us (35%)
  Pallas kernels  5.44 us (10%)
  local copies, waits for them, and re-layouts  1.59 us (3%)
  waiting for transfers between devices  1.17 us (2%)
  between operations  0.68 us (1%)
    all_to_all x2, blocking collectives, exchange(): lax.all_to_all(copies, axes, 0, 0, tiled=True, axis_index_groups=[order])  27.3 us
    all_to_all x1, starting transfers between devices, exchange(): lax.all_to_all(copies, axes, 0, 0, tiled=True, axis_index_groups=[order])  19.8 us
    pallas_call x5, Pallas kernels, call(): pl.pallas_call(kernel, out_shape=out_shape, in_specs=[hbm if at in fetche...  5.44 us
    unnamed x3, local copies, waits for them, and re-layouts  1.59 us
    all_to_all x1, waiting for transfers between devices, exchange(): lax.all_to_all(copies, axes, 0, 0, tiled=True, axis_index_groups=[order])  1.17 us
  transfers between devices with their start and end apart: 1, of which 1 were waited for; matrix products, arithmetic and copies ran while one was open for 0% of the time, Pallas kernels for 1%

profile of v4, /device:TPU:1, one launch (start us, length us, event | category | flops | bytes accessed | tf_op | source)
XLA Modules:
  0.0 56.0 jit_solution(3628423170154136610)
XLA Ops:
  0.6 1.4 %shard_map.58 = f32[32,1,384]{2,1,0:T(1,128)} custom-call(f32[1,8,24]{2,1,0:T(8,128)} %two_hbm.1, f32[1,4,24]{2,1,0:T(4,128)} %three_hbm.1), custom_call_target="tpu_custom_call" | custom-call | tf_op jit(solution)/shard_map/pallas_call | solution.py:39
  2.1 19.8 %all-to-all-start = ((f32[32,1,384]{2,1,0:T(1,128)}), f32[32,1,384]{2,1,0:T(1,128)S(1)}, u32[]{:S(2)}, u32[]{:S(2)}) async-start(f32[32,1,384]{2,1,0:T(1,128)} %shard_map.58), calls=%async_computation | async-start | bytes 98304 | tf_op jit(solution)/shard_map/all_to_all | solution.py:29
  21.9 0.0 copy-start
  21.9 1.6 %copy-done = f32[16,256,128]{2,1,0:T(8,128)S(1)} copy-done((f32[16,256,128]{2,1,0:T(8,128)S(1)}, f32[16,256,128]{2,1,0:T(8,128)}, u32[]{:S(2)}) %copy-start) | copy-done | bytes 2097176
  23.5 0.8 %shard_map.59 = (bf16[16,256,256]{2,1,0:T(8,128)(2,1)S(1)}, bf16[8,256,256]{2,1,0:T(8,128)(2,1)S(1)}) custom-call(f32[16,256,128]{2,1,0:T(8,128)S(1)} %copy-done), custom_call_target="tpu_custom_call" | custom-call | flops 2621440 | bytes 5242880 | tf_op jit(solution)/shard_map/pallas_call | solution.py:39
  24.3 1.2 %all-to-all-done = f32[32,1,384]{2,1,0:T(1,128)S(1)} async-done(((f32[32,1,384]{2,1,0:T(1,128)}), f32[32,1,384]{2,1,0:T(1,128)S(1)}, u32[]{:S(2)}, u32[]{:S(2)}) %all-to-all-start) | async-done | bytes 49184 | tf_op jit(solution)/shard_map/all_to_all | solution.py:29
  25.5 1.3 %shard_map.60 = f32[32,8,96]{2,1,0:T(8,128)S(1)} custom-call(f32[32,384]{1,0:T(8,128)S(1)} %bitcast.4, bf16[16,256,256]{2,1,0:T(8,128)(2,1)S(1)} %get-tuple-element.10.upper_ref, bf16[8,256,256]{2,1,0:T(8,128)(2,1)S(1)} %get-tuple-element.11.low_ref), custom_call_target="tpu_custom_call" | custom-call | tf_op jit(solution)/shard_map/pallas_call | solution.py:39
  26.8 11.4 %all_to_all.15.parts_ref = f32[32,8,96]{2,1,0:T(8,128)S(1)} all-to-all(f32[32,8,96]{2,1,0:T(8,128)S(1)} %shard_map.60), channel_id=1, replica_groups={{26,27,24,25,30,31,28,29,18,19,16,17,22,23,20,21,10,11,8,9,14,15,12,13,..., dimensions={0} | all-to-all | bytes 196608 | tf_op jit(solution)/shard_map/all_to_all | solution.py:29
  38.2 1.1 %shard_map.61 = (f32[16,8,72]{2,1,0:T(8,128)S(1)}, f32[16,24]{1,0:T(8,128)S(1)}) custom-call(f32[32,8,96]{2,1,0:T(8,128)S(1)} %all_to_all.15.parts_ref), custom_call_target="tpu_custom_call" | custom-call | tf_op jit(solution)/shard_map/pallas_call | solution.py:39
  39.3 15.9 %all_to_all.16.grams_ref = f32[16,8,72]{2,1,0:T(8,128)S(1)} all-to-all(f32[16,8,72]{2,1,0:T(8,128)S(1)} %get-tuple-element.12), channel_id=1, replica_groups={{256,288,320,352,384,416,448,480,0,32,64,96,128,160,192,224},{257,289,3..., dimensions={0} | all-to-all | bytes 73728 | tf_op jit(solution)/shard_map/all_to_all | solution.py:29
  55.2 0.8 %shard_map.62 = (f32[16,24]{1,0:T(8,128)}, f32[1,24]{1,0:T(1,128)}, f32[24,24]{1,0:T(8,128)}) custom-call(f32[16,8,72]{2,1,0:T(8,128)S(1)} %all_to_all.16.grams_ref, f32[16,24]{1,0:T(8,128)S(1)} %get-tuple-element.13.updated_ref), custom_call_target="tpu_custom_call" | custom-call | tf_op jit(solution)/shard_map/pallas_call | solution.py:39
  (1 shorter events, 0.0 us)
Async XLA Ops:
  2.1 23.4 %all-to-all-start = ((f32[32,1,384]{2,1,0:T(1,128)}), f32[32,1,384]{2,1,0:T(1,128)S(1)}, u32[]{:S(2)}, u32[]{:S(2)}) async-start(f32[32,1,384]{2,1,0:T(1,128)} %shard_map.58), calls=%async_computation | async-start | bytes 98304 | tf_op jit(solution)/shard_map/all_to_all | solution.py:29
  21.9 1.6 %copy-start = (f32[16,256,128]{2,1,0:T(8,128)S(1)}, f32[16,256,128]{2,1,0:T(8,128)}, u32[]{:S(2)}) copy-start(f32[16,256,128]{2,1,0:T(8,128)} %tensor_ref.1) | copy-start | bytes 6291460

commit v5 on v4

--- a/solution.py
+++ b/solution.py
@@ -95,7 +95,7 @@
     return fold_gram(full, rank)
 
 
-def split_kernel(tensor_ref, upper_ref, low_ref):
+def split_kernel(tensor_ref, split_ref):
     width = tensor_ref.shape[-1]
 
     @pl.loop(0, tensor_ref.shape[0])
@@ -104,18 +104,9 @@
         high = cells.astype(jnp.bfloat16)
         rest = cells - high.astype(jnp.float32)
         middle = rest.astype(jnp.bfloat16)
-        upper_ref[row, :, :width] = high
-        upper_ref[row, :, width:] = middle
-        low = (rest - middle.astype(jnp.float32)).astype(jnp.bfloat16)
-        half = tensor_ref.shape[0] // 2
-
-        @pl.when(row < half)
-        def _():
-            low_ref[row, :, :width] = low
-
-        @pl.when(row >= half)
-        def _():
-            low_ref[row - half, :, width:] = low
+        split_ref[row, :, :width] = high
+        split_ref[row, :, width : 2 * width] = middle
+        split_ref[row, :, 2 * width :] = (rest - middle.astype(jnp.float32)).astype(jnp.bfloat16)
 
 
 def runs_from(start, size):
@@ -123,7 +114,7 @@
 
 
 def contract_kernel(
-    gathered_ref, upper_ref, low_ref, out_ref, two_ref, three_ref, sums_ref,
+    gathered_ref, split_ref, out_ref, two_ref, three_ref, sums_ref,
     gram_two_ref, gram_three_ref, *, rank, cores, chips, starts
 ):
     count_two = two_ref.shape[0] // (cores * chips)
@@ -142,20 +133,10 @@
                 ref[pl.ds(row, run, stride=count * cores), :] = thrice
     two = two_ref[...]
     parts_three = parts_of(three_ref[...], rank)
-    double = jnp.concatenate([parts_three, parts_three], axis=0)
-    blank = jnp.zeros((parts_three.shape[0], LANES - parts_three.shape[1]), jnp.bfloat16)
-    padded = jnp.concatenate([parts_three, blank], axis=1)
-    empty = jnp.zeros_like(padded)
-    diagonal = jnp.concatenate(
-        [jnp.concatenate([padded, empty], axis=1), jnp.concatenate([empty, padded], axis=1)], axis=0
-    )
-    half = low_ref.shape[0]
-    for row in range(half):
-        lows = jnp.dot(low_ref[row], diagonal, preferred_element_type=jnp.float32)
-        for each, lane in ((row, 0), (row + half, LANES)):
-            through = jnp.dot(upper_ref[each], double, preferred_element_type=jnp.float32)
-            through += lows[:, lane : lane + 3 * rank]
-            sums_ref[each : each + 1, :] = jnp.sum(through * two, axis=0, keepdims=True)
+    stacked = jnp.concatenate([parts_three, parts_three, parts_three], axis=0)
+    for row in range(split_ref.shape[0]):
+        through = jnp.dot(split_ref[row], stacked, preferred_element_type=jnp.float32)
+        sums_ref[row : row + 1, :] = jnp.sum(through * two, axis=0, keepdims=True)
     partial = fold_lanes(sums_ref[...], rank).T
     gram_two_ref[...] = gram_of_parts(parts_of(two, rank), rank)
     gram_three_ref[...] = gram_of_parts(parts_three, rank)
@@ -289,16 +270,13 @@
         third_factor,
         fetched=(0, 1),
     )
-    rows_from = (cores - 1, chips // 2)
+    rows_from = (cores - 1, 5 * chips // 8)
     plane_from = (cores - 1, groups_two // 2, groups_three // 2)
     gathered = exchange(packed, ("core", "z"), rows_from).reshape(members, width)
 
-    upper, low = call(
+    split = call(
         split_kernel,
-        (
-            jax.ShapeDtypeStruct((*tensor.shape[:2], 2 * tensor.shape[2]), jnp.bfloat16),
-            jax.ShapeDtypeStruct((rows // 2, tensor.shape[1], 2 * tensor.shape[2]), jnp.bfloat16),
-        ),
+        jax.ShapeDtypeStruct((*tensor.shape[:2], 3 * tensor.shape[2]), jnp.bfloat16),
         [],
         tensor,
         cost=pl.CostEstimate(flops=5 * tensor.size, bytes_accessed=10 * tensor.size, transcendentals=0),
@@ -314,8 +292,7 @@
             pltpu.VMEM((rank, rank), f32),
         ],
         gathered,
-        upper,
-        low,
+        split,
     )
     parts = exchange(messages, ("core", "ja", "ka"), plane_from)
 
@@ -336,7 +313,7 @@
         [pltpu.VMEM((cores * rows, rank), f32)],
         parts,
     )
-    grams = exchange(grams, ("z",), (chips // 2,))
+    grams = exchange(grams, ("z",), (chips // 2 + 1,))
 
     factor, column_rms, correlation = call(
         functools.partial(scale_kernel, rank=rank, total_rows=total_rows),

time: 56.3 us -> 55.4 us (0.984)
  waiting for transfers between devices: 1.17 us -> 3.08 us
  starting transfers between devices: 19.8 us -> 18 us
  blocking collectives: 27.3 us -> 26.5 us
    all_to_all x1, waiting for transfers between devices: 1.17 us -> 3.08 us  [exchange(): lax.all_to_all(copies, axes, 0, 0, tiled=True, axis_index_groups=[order])]
    all_to_all x1, starting transfers between devices: 19.8 us -> 18 us  [exchange(): lax.all_to_all(copies, axes, 0, 0, tiled=True, axis_index_groups=[order])]
    all_to_all x2, blocking collectives: 27.3 us -> 26.5 us  [exchange(): lax.all_to_all(copies, axes, 0, 0, tiled=True, axis_index_groups=[order])]
where the time goes in v5:
time: 55.4 us; the launch traced here: 55.1 us
  blocking collectives  26.5 us (48%)
  starting transfers between devices  18 us (32%)
  Pallas kernels  5.26 us (9%)
  waiting for transfers between devices  3.08 us (6%)
  local copies, waits for them, and re-layouts  1.59 us (3%)
  between operations  0.68 us (1%)
    all_to_all x2, blocking collectives, exchange(): lax.all_to_all(copies, axes, 0, 0, tiled=True, axis_index_groups=[order])  26.5 us
    all_to_all x1, starting transfers between devices, exchange(): lax.all_to_all(copies, axes, 0, 0, tiled=True, axis_index_groups=[order])  18 us
    pallas_call x5, Pallas kernels, call(): pl.pallas_call(kernel, out_shape=out_shape, in_specs=[hbm if at in fetche...  5.26 us
    all_to_all x1, waiting for transfers between devices, exchange(): lax.all_to_all(copies, axes, 0, 0, tiled=True, axis_index_groups=[order])  3.08 us
    unnamed x3, local copies, waits for them, and re-layouts  1.59 us
  transfers between devices with their start and end apart: 1, of which 1 were waited for; matrix products, arithmetic and copies ran while one was open for 0% of the time, Pallas kernels for 1%

profile of v5, /device:TPU:1, one launch (start us, length us, event | category | flops | bytes accessed | tf_op | source)
XLA Modules:
  0.0 55.1 jit_solution(8891061069816580840)
XLA Ops:
  0.6 1.4 %shard_map.58 = f32[32,1,384]{2,1,0:T(1,128)} custom-call(f32[1,8,24]{2,1,0:T(8,128)} %two_hbm.1, f32[1,4,24]{2,1,0:T(4,128)} %three_hbm.1), custom_call_target="tpu_custom_call" | custom-call | tf_op jit(solution)/shard_map/pallas_call | solution.py:39
  2.1 18.0 %all-to-all-start = ((f32[32,1,384]{2,1,0:T(1,128)}), f32[32,1,384]{2,1,0:T(1,128)S(1)}, u32[]{:S(2)}, u32[]{:S(2)}) async-start(f32[32,1,384]{2,1,0:T(1,128)} %shard_map.58), calls=%async_computation | async-start | bytes 98304 | tf_op jit(solution)/shard_map/all_to_all | solution.py:29
  20.1 0.0 copy-start
  20.1 1.6 %copy-done = f32[16,256,128]{2,1,0:T(8,128)S(1)} copy-done((f32[16,256,128]{2,1,0:T(8,128)S(1)}, f32[16,256,128]{2,1,0:T(8,128)}, u32[]{:S(2)}) %copy-start) | copy-done | bytes 2097176
  21.7 0.6 %shard_map.59.split_ref = bf16[16,256,384]{2,1,0:T(8,128)(2,1)S(1)} custom-call(f32[16,256,128]{2,1,0:T(8,128)S(1)} %copy-done), custom_call_target="tpu_custom_call" | custom-call | flops 2621440 | bytes 5242880 | tf_op jit(solution)/shard_map/pallas_call | solution.py:39
  22.3 3.1 %all-to-all-done = f32[32,1,384]{2,1,0:T(1,128)S(1)} async-done(((f32[32,1,384]{2,1,0:T(1,128)}), f32[32,1,384]{2,1,0:T(1,128)S(1)}, u32[]{:S(2)}, u32[]{:S(2)}) %all-to-all-start) | async-done | bytes 49184 | tf_op jit(solution)/shard_map/all_to_all | solution.py:29
  25.4 1.3 %shard_map.60 = f32[32,8,96]{2,1,0:T(8,128)S(1)} custom-call(f32[32,384]{1,0:T(8,128)S(1)} %bitcast.4, bf16[16,256,384]{2,1,0:T(8,128)(2,1)S(1)} %shard_map.59.split_ref), custom_call_target="tpu_custom_call" | custom-call | tf_op jit(solution)/shard_map/pallas_call | solution.py:39
  26.8 11.4 %all_to_all.15.parts_ref = f32[32,8,96]{2,1,0:T(8,128)S(1)} all-to-all(f32[32,8,96]{2,1,0:T(8,128)S(1)} %shard_map.60), channel_id=1, replica_groups={{26,27,24,25,30,31,28,29,18,19,16,17,22,23,20,21,10,11,8,9,14,15,12,13,..., dimensions={0} | all-to-all | bytes 196608 | tf_op jit(solution)/shard_map/all_to_all | solution.py:29
  38.2 1.1 %shard_map.61 = (f32[16,8,72]{2,1,0:T(8,128)S(1)}, f32[16,24]{1,0:T(8,128)S(1)}) custom-call(f32[32,8,96]{2,1,0:T(8,128)S(1)} %all_to_all.15.parts_ref), custom_call_target="tpu_custom_call" | custom-call | tf_op jit(solution)/shard_map/pallas_call | solution.py:39
  39.3 15.1 %all_to_all.16.grams_ref = f32[16,8,72]{2,1,0:T(8,128)S(1)} all-to-all(f32[16,8,72]{2,1,0:T(8,128)S(1)} %get-tuple-element.8), channel_id=1, replica_groups={{288,320,352,384,416,448,480,0,32,64,96,128,160,192,224,256},{289,321,3..., dimensions={0} | all-to-all | bytes 73728 | tf_op jit(solution)/shard_map/all_to_all | solution.py:29
  54.3 0.8 %shard_map.62 = (f32[16,24]{1,0:T(8,128)}, f32[1,24]{1,0:T(1,128)}, f32[24,24]{1,0:T(8,128)}) custom-call(f32[16,8,72]{2,1,0:T(8,128)S(1)} %all_to_all.16.grams_ref, f32[16,24]{1,0:T(8,128)S(1)} %get-tuple-element.9.updated_ref), custom_call_target="tpu_custom_call" | custom-call | tf_op jit(solution)/shard_map/pallas_call | solution.py:39
  (1 shorter events, 0.0 us)
Async XLA Ops:
  2.1 23.4 %all-to-all-start = ((f32[32,1,384]{2,1,0:T(1,128)}), f32[32,1,384]{2,1,0:T(1,128)S(1)}, u32[]{:S(2)}, u32[]{:S(2)}) async-start(f32[32,1,384]{2,1,0:T(1,128)} %shard_map.58), calls=%async_computation | async-start | bytes 98304 | tf_op jit(solution)/shard_map/all_to_all | solution.py:29
  20.1 1.6 %copy-start = (f32[16,256,128]{2,1,0:T(8,128)S(1)}, f32[16,256,128]{2,1,0:T(8,128)}, u32[]{:S(2)}) copy-start(f32[16,256,128]{2,1,0:T(8,128)} %tensor_ref.1) | copy-start | bytes 6291460

commit v6 on v5

--- a/solution.py
+++ b/solution.py
@@ -12,6 +12,7 @@
 EPSILON = 1e-06
 LANES = 128
 SUBLANES = 8
+QUAD = 4
 BLOCK = 12
 VMEM_BYTES = 8 * 2**20
 
@@ -147,6 +148,30 @@
     pieces.append(gram_two_ref[pl.ds(pl.multiple_of(tile_two, SUBLANES), SUBLANES), :])
     pieces.append(gram_three_ref[pl.ds(pl.multiple_of(tile_three, SUBLANES), SUBLANES), :])
     out_ref[...] = jnp.broadcast_to(jnp.concatenate(pieces, axis=1)[None], out_ref.shape)
+
+
+def upper_spans(rank):
+    return [(first, sum(rank - f for f in range(0, first, QUAD))) for first in range(0, rank, QUAD)]
+
+
+def upper_width(rank):
+    return sum(rank - first for first in range(0, rank, QUAD))
+
+
+def upper_rows(full):
+    rank = full.shape[0]
+    return jnp.concatenate([full[f : f + QUAD, f:] for f, _ in upper_spans(rank)], axis=1)
+
+
+def from_upper_rows(packed, rank):
+    rows = []
+    for first, at in upper_spans(rank):
+        piece = packed[:, at : at + rank - first]
+        rows.append(jnp.concatenate([jnp.zeros((QUAD, first), jnp.float32), piece], axis=1) if first else piece)
+    upper = jnp.concatenate(rows, axis=0)
+    down = lax.broadcasted_iota(jnp.int32, upper.shape, 0) // QUAD
+    right = lax.broadcasted_iota(jnp.int32, upper.shape, 1) // QUAD
+    return jnp.where(down > right, upper.T, upper)
 
 
 def across_sublanes(tile, sublane):
@@ -220,17 +245,14 @@
         stacked, stacked, (((1,), (1,)), ((), ())), preferred_element_type=jnp.float32
     )
     gram = fold_gram(full, rank)
-    pieces = [gram[SUBLANES * t : SUBLANES * (t + 1)] for t in range(tiles)]
-    out_ref[...] = jnp.broadcast_to(jnp.concatenate(pieces, axis=1)[None], out_ref.shape)
+    out_ref[...] = jnp.broadcast_to(upper_rows(gram)[None], out_ref.shape)
 
 
 def scale_kernel(grams_ref, updated_ref, factor_ref, rms_ref, correlation_ref, *, rank, total_rows):
     total = grams_ref[0]
     for source in range(1, grams_ref.shape[0]):
         total += grams_ref[source]
-    gram = jnp.concatenate(
-        [total[:, rank * t : rank * (t + 1)] for t in range(rank // SUBLANES)], axis=0
-    )
+    gram = from_upper_rows(total, rank)
     diagonal = jnp.where(
         lax.broadcasted_iota(jnp.int32, gram.shape, 0) == lax.broadcasted_iota(jnp.int32, gram.shape, 1),
         gram,
@@ -307,7 +329,7 @@
             starts=plane_from,
         ),
         (
-            jax.ShapeDtypeStruct((chips, SUBLANES, tiles * rank), f32),
+            jax.ShapeDtypeStruct((chips, QUAD, upper_width(rank)), f32),
             jax.ShapeDtypeStruct((rows, rank), f32),
         ),
         [pltpu.VMEM((cores * rows, rank), f32)],

time: 55.4 us -> 54.3 us (0.980)
  blocking collectives: 26.5 us -> 25.3 us
    all_to_all x2, blocking collectives: 26.5 us -> 25.3 us  [exchange(): lax.all_to_all(copies, axes, 0, 0, tiled=True, axis_index_groups=[order])]
where the time goes in v6:
time: 54.3 us; the launch traced here: 54 us
  blocking collectives  25.3 us (47%)
  starting transfers between devices  18 us (33%)
  Pallas kernels  5.34 us (10%)
  waiting for transfers between devices  3.08 us (6%)
  local copies, waits for them, and re-layouts  1.59 us (3%)
  between operations  0.67 us (1%)
    all_to_all x2, blocking collectives, exchange(): lax.all_to_all(copies, axes, 0, 0, tiled=True, axis_index_groups=[order])  25.3 us
    all_to_all x1, starting transfers between devices, exchange(): lax.all_to_all(copies, axes, 0, 0, tiled=True, axis_index_groups=[order])  18 us
    pallas_call x5, Pallas kernels, call(): pl.pallas_call(kernel, out_shape=out_shape, in_specs=[hbm if at in fetche...  5.34 us
    all_to_all x1, waiting for transfers between devices, exchange(): lax.all_to_all(copies, axes, 0, 0, tiled=True, axis_index_groups=[order])  3.08 us
    unnamed x3, local copies, waits for them, and re-layouts  1.59 us
  transfers between devices with their start and end apart: 1, of which 1 were waited for; matrix products, arithmetic and copies ran while one was open for 0% of the time, Pallas kernels for 1%

profile of v6, /device:TPU:1, one launch (start us, length us, event | category | flops | bytes accessed | tf_op | source)
XLA Modules:
  0.0 54.0 jit_solution(11113070004262974396)
XLA Ops:
  0.6 1.4 %shard_map.58 = f32[32,1,384]{2,1,0:T(1,128)} custom-call(f32[1,8,24]{2,1,0:T(8,128)} %two_hbm.1, f32[1,4,24]{2,1,0:T(4,128)} %three_hbm.1), custom_call_target="tpu_custom_call" | custom-call | tf_op jit(solution)/shard_map/pallas_call | solution.py:40
  2.1 18.0 %all-to-all-start = ((f32[32,1,384]{2,1,0:T(1,128)}), f32[32,1,384]{2,1,0:T(1,128)S(1)}, u32[]{:S(2)}, u32[]{:S(2)}) async-start(f32[32,1,384]{2,1,0:T(1,128)} %shard_map.58), calls=%async_computation | async-start | bytes 98304 | tf_op jit(solution)/shard_map/all_to_all | solution.py:30
  20.1 0.0 copy-start
  20.1 1.6 %copy-done = f32[16,256,128]{2,1,0:T(8,128)S(1)} copy-done((f32[16,256,128]{2,1,0:T(8,128)S(1)}, f32[16,256,128]{2,1,0:T(8,128)}, u32[]{:S(2)}) %copy-start) | copy-done | bytes 2097176
  21.7 0.6 %shard_map.59.split_ref = bf16[16,256,384]{2,1,0:T(8,128)(2,1)S(1)} custom-call(f32[16,256,128]{2,1,0:T(8,128)S(1)} %copy-done), custom_call_target="tpu_custom_call" | custom-call | flops 2621440 | bytes 5242880 | tf_op jit(solution)/shard_map/pallas_call | solution.py:40
  22.3 3.1 %all-to-all-done = f32[32,1,384]{2,1,0:T(1,128)S(1)} async-done(((f32[32,1,384]{2,1,0:T(1,128)}), f32[32,1,384]{2,1,0:T(1,128)S(1)}, u32[]{:S(2)}, u32[]{:S(2)}) %all-to-all-start) | async-done | bytes 49184 | tf_op jit(solution)/shard_map/all_to_all | solution.py:30
  25.4 1.3 %shard_map.60 = f32[32,8,96]{2,1,0:T(8,128)S(1)} custom-call(f32[32,384]{1,0:T(8,128)S(1)} %bitcast.4, bf16[16,256,384]{2,1,0:T(8,128)(2,1)S(1)} %shard_map.59.split_ref), custom_call_target="tpu_custom_call" | custom-call | tf_op jit(solution)/shard_map/pallas_call | solution.py:40
  26.8 11.4 %all_to_all.15.parts_ref = f32[32,8,96]{2,1,0:T(8,128)S(1)} all-to-all(f32[32,8,96]{2,1,0:T(8,128)S(1)} %shard_map.60), channel_id=1, replica_groups={{26,27,24,25,30,31,28,29,18,19,16,17,22,23,20,21,10,11,8,9,14,15,12,13,..., dimensions={0} | all-to-all | bytes 196608 | tf_op jit(solution)/shard_map/all_to_all | solution.py:30
  38.2 1.1 %shard_map.61 = (f32[16,4,84]{2,1,0:T(4,128)S(1)}, f32[16,24]{1,0:T(8,128)S(1)}) custom-call(f32[32,8,96]{2,1,0:T(8,128)S(1)} %all_to_all.15.parts_ref), custom_call_target="tpu_custom_call" | custom-call | tf_op jit(solution)/shard_map/pallas_call | solution.py:40
  39.3 13.9 %all_to_all.16.grams_ref = f32[16,4,84]{2,1,0:T(4,128)S(1)} all-to-all(f32[16,4,84]{2,1,0:T(4,128)S(1)} %get-tuple-element.8), channel_id=1, replica_groups={{288,320,352,384,416,448,480,0,32,64,96,128,160,192,224,256},{289,321,3..., dimensions={0} | all-to-all | bytes 43008 | tf_op jit(solution)/shard_map/all_to_all | solution.py:30
  53.1 0.9 %shard_map.62 = (f32[16,24]{1,0:T(8,128)}, f32[1,24]{1,0:T(1,128)}, f32[24,24]{1,0:T(8,128)}) custom-call(f32[16,4,84]{2,1,0:T(4,128)S(1)} %all_to_all.16.grams_ref, f32[16,24]{1,0:T(8,128)S(1)} %get-tuple-element.9.updated_ref), custom_call_target="tpu_custom_call" | custom-call | tf_op jit(solution)/shard_map/pallas_call | solution.py:40
  (1 shorter events, 0.0 us)
Async XLA Ops:
  2.1 23.4 %all-to-all-start = ((f32[32,1,384]{2,1,0:T(1,128)}), f32[32,1,384]{2,1,0:T(1,128)S(1)}, u32[]{:S(2)}, u32[]{:S(2)}) async-start(f32[32,1,384]{2,1,0:T(1,128)} %shard_map.58), calls=%async_computation | async-start | bytes 98304 | tf_op jit(solution)/shard_map/all_to_all | solution.py:30
  20.1 1.6 %copy-start = (f32[16,256,128]{2,1,0:T(8,128)S(1)}, f32[16,256,128]{2,1,0:T(8,128)}, u32[]{:S(2)}) copy-start(f32[16,256,128]{2,1,0:T(8,128)} %tensor_ref.1) | copy-start | bytes 6291460

commit v7 on v6

--- a/solution.py
+++ b/solution.py
@@ -21,13 +21,15 @@
     return [(start + step) % size for step in range(size)]
 
 
-def exchange(copies, axes, starts):
+def upper_first(start, size):
+    half = size // 2
+    return [half + at for at in counted_from(start - half, half)] + list(range(half))
+
+
+def exchange(copies, axes, orders):
     sizes = [lax.axis_size(axis) for axis in axes]
-    order = [
-        int(np.ravel_multi_index(member, sizes))
-        for member in itertools.product(*map(counted_from, starts, sizes))
-    ]
-    return lax.all_to_all(copies, axes, 0, 0, tiled=True, axis_index_groups=[order])
+    listed = [int(np.ravel_multi_index(member, sizes)) for member in itertools.product(*orders)]
+    return lax.all_to_all(copies, axes, 0, 0, tiled=True, axis_index_groups=[listed])
 
 
 def lane_start(slot, rank):
@@ -110,19 +112,21 @@
         split_ref[row, :, 2 * width :] = (rest - middle.astype(jnp.float32)).astype(jnp.bfloat16)
 
 
-def runs_from(start, size):
-    return [(0, start, size - start)] + ([(size - start, 0, start)] if start else [])
-
-
 def contract_kernel(
     gathered_ref, split_ref, out_ref, two_ref, three_ref, sums_ref,
-    gram_two_ref, gram_three_ref, *, rank, cores, chips, starts
+    gram_two_ref, gram_three_ref, *, rank, orders
 ):
+    cores, chips = map(len, orders)
     count_two = two_ref.shape[0] // (cores * chips)
     count_three = three_ref.shape[0] // (cores * chips)
-    for at, core in enumerate(counted_from(starts[0], cores)):
-        for first, chip, run in runs_from(starts[1], chips):
-            block = gathered_ref[at * chips + first : at * chips + first + run, :]
+    half = chips // 2
+    for at, core in enumerate(orders[0]):
+        for first in range(0, chips, half):
+            block = gathered_ref[at * chips + first : at * chips + first + half, :]
+            chip = min(orders[1][first : first + half])
+            turn = orders[1].index(chip) - first
+            if turn:
+                block = jnp.concatenate([block[turn:], block[:turn]], axis=0)
             for slot in range(count_two + count_three):
                 start = lane_start(slot, rank)
                 piece = block[:, start : start + rank]
@@ -131,7 +135,7 @@
                     (two_ref, count_two, slot) if slot < count_two else (three_ref, count_three, slot - count_two)
                 )
                 row += count * (cores * chip + core)
-                ref[pl.ds(row, run, stride=count * cores), :] = thrice
+                ref[pl.ds(row, half, stride=count * cores), :] = thrice
     two = two_ref[...]
     parts_three = parts_of(three_ref[...], rank)
     stacked = jnp.concatenate([parts_three, parts_three, parts_three], axis=0)
@@ -192,11 +196,18 @@
 
     for begin in range(0, rank, BLOCK):
         columns = [[across_lanes(v, begin + m) for v in tiles] for m in range(BLOCK)]
+        pivot = across_sublanes(columns[0][begin // SUBLANES], begin % SUBLANES)
         for m in range(BLOCK):
             t, s = divmod(begin + m, SUBLANES)
             column = columns[m]
-            inverse = 1.0 / across_sublanes(column[t], s)
+            inverse = 1.0 / pivot
             pivot_row = across_sublanes(tiles[t], s) * inverse
+            if m + 1 < BLOCK:
+                after = columns[m + 1]
+                entry = across_sublanes(after[t], s) * inverse
+                t_after, s_after = divmod(begin + m + 1, SUBLANES)
+                pivot = across_sublanes(after[t_after], s_after)
+                pivot -= across_sublanes(column[t_after], s_after) * entry
             tiles = reduced(tiles, column, pivot_row, t, s)
             for later in range(m + 1, BLOCK):
                 entry = across_sublanes(columns[later][t], s) * inverse
@@ -204,18 +215,14 @@
     return tiles
 
 
-def solve_kernel(parts_ref, out_ref, updated_ref, chip_ref, *, rank, rows, cores, groups_two, groups_three, starts):
+def solve_kernel(parts_ref, out_ref, updated_ref, chip_ref, *, rank, rows, orders):
     tiles = rank // SUBLANES
+    cores, groups_two, groups_three = map(len, orders)
     group = groups_two * groups_three
-    place = {
-        member: at
-        for at, member in enumerate(
-            itertools.product(*map(counted_from, starts, (cores, groups_two, groups_three)))
-        )
-    }
+    place = {member: at for at, member in enumerate(itertools.product(*orders))}
     products = []
     for core in range(cores):
-        first = place[core, starts[1], starts[2]]
+        first = place[core, orders[1][0], orders[2][0]]
         total = parts_ref[first]
         for source in range(1, group):
             total += parts_ref[first + source]
@@ -292,9 +299,15 @@
         third_factor,
         fetched=(0, 1),
     )
-    rows_from = (cores - 1, 5 * chips // 8)
-    plane_from = (cores - 1, groups_two // 2, groups_three // 2)
-    gathered = exchange(packed, ("core", "z"), rows_from).reshape(members, width)
+    cores_order = counted_from(cores - 1, cores)
+    rows_order = (cores_order, upper_first(5 * chips // 8, chips))
+    plane_order = (
+        cores_order,
+        counted_from(groups_two // 2, groups_two),
+        counted_from(groups_three // 2, groups_three),
+    )
+    chips_order = (counted_from(chips // 2 + 1, chips),)
+    gathered = exchange(packed, ("core", "z"), rows_order).reshape(members, width)
 
     split = call(
         split_kernel,
@@ -304,7 +317,7 @@
         cost=pl.CostEstimate(flops=5 * tensor.size, bytes_accessed=10 * tensor.size, transcendentals=0),
     )
     messages = call(
-        functools.partial(contract_kernel, rank=rank, cores=cores, chips=chips, starts=rows_from),
+        functools.partial(contract_kernel, rank=rank, orders=rows_order),
         jax.ShapeDtypeStruct((cores * groups_two * groups_three, SUBLANES, tiles * rows + 2 * rank), f32),
         [
             pltpu.VMEM((tensor.shape[1], 3 * rank), f32),
@@ -316,18 +329,10 @@
         gathered,
         split,
     )
-    parts = exchange(messages, ("core", "ja", "ka"), plane_from)
+    parts = exchange(messages, ("core", "ja", "ka"), plane_order)
 
     grams, updated = call(
-        functools.partial(
-            solve_kernel,
-            rank=rank,
-            rows=rows,
-            cores=cores,
-            groups_two=groups_two,
-            groups_three=groups_three,
-            starts=plane_from,
-        ),
+        functools.partial(solve_kernel, rank=rank, rows=rows, orders=plane_order),
         (
             jax.ShapeDtypeStruct((chips, QUAD, upper_width(rank)), f32),
             jax.ShapeDtypeStruct((rows, rank), f32),
@@ -335,7 +340,7 @@
         [pltpu.VMEM((cores * rows, rank), f32)],
         parts,
     )
-    grams = exchange(grams, ("z",), (chips // 2 + 1,))
+    grams = exchange(grams, ("z",), chips_order)
 
     factor, column_rms, correlation = call(
         functools.partial(scale_kernel, rank=rank, total_rows=total_rows),

time: 54.3 us -> 54.2 us (level)
  no operation moved by 1% of the time
where the time goes in v7:
time: 54.2 us; the launch traced here: 53.9 us
  blocking collectives  25.3 us (47%)
  starting transfers between devices  18 us (33%)
  Pallas kernels  5.3 us (10%)
  waiting for transfers between devices  3.09 us (6%)
  local copies, waits for them, and re-layouts  1.59 us (3%)
  between operations  0.67 us (1%)
    all_to_all x2, blocking collectives, exchange(): lax.all_to_all(copies, axes, 0, 0, tiled=True, axis_index_groups=[listed])  25.3 us
    all_to_all x1, starting transfers between devices, exchange(): lax.all_to_all(copies, axes, 0, 0, tiled=True, axis_index_groups=[listed])  18 us
    pallas_call x5, Pallas kernels, call(): pl.pallas_call(kernel, out_shape=out_shape, in_specs=[hbm if at in fetche...  5.3 us
    all_to_all x1, waiting for transfers between devices, exchange(): lax.all_to_all(copies, axes, 0, 0, tiled=True, axis_index_groups=[listed])  3.09 us
    unnamed x3, local copies, waits for them, and re-layouts  1.59 us
  transfers between devices with their start and end apart: 1, of which 1 were waited for; matrix products, arithmetic and copies ran while one was open for 0% of the time, Pallas kernels for 1%

profile of v7, /device:TPU:1, one launch (start us, length us, event | category | flops | bytes accessed | tf_op | source)
XLA Modules:
  0.0 53.9 jit_solution(3439503949763067236)
XLA Ops:
  0.6 1.4 %shard_map.58 = f32[32,1,384]{2,1,0:T(1,128)} custom-call(f32[1,8,24]{2,1,0:T(8,128)} %two_hbm.1, f32[1,4,24]{2,1,0:T(4,128)} %three_hbm.1), custom_call_target="tpu_custom_call" | custom-call | tf_op jit(solution)/shard_map/pallas_call | solution.py:42
  2.1 18.0 %all-to-all-start = ((f32[32,1,384]{2,1,0:T(1,128)}), f32[32,1,384]{2,1,0:T(1,128)S(1)}, u32[]{:S(2)}, u32[]{:S(2)}) async-start(f32[32,1,384]{2,1,0:T(1,128)} %shard_map.58), calls=%async_computation | async-start | bytes 98304 | tf_op jit(solution)/shard_map/all_to_all | solution.py:32
  20.1 0.0 copy-start
  20.1 1.6 %copy-done = f32[16,256,128]{2,1,0:T(8,128)S(1)} copy-done((f32[16,256,128]{2,1,0:T(8,128)S(1)}, f32[16,256,128]{2,1,0:T(8,128)}, u32[]{:S(2)}) %copy-start) | copy-done | bytes 2097176
  21.7 0.6 %shard_map.59.split_ref = bf16[16,256,384]{2,1,0:T(8,128)(2,1)S(1)} custom-call(f32[16,256,128]{2,1,0:T(8,128)S(1)} %copy-done), custom_call_target="tpu_custom_call" | custom-call | flops 2621440 | bytes 5242880 | tf_op jit(solution)/shard_map/pallas_call | solution.py:42
  22.3 3.1 %all-to-all-done = f32[32,1,384]{2,1,0:T(1,128)S(1)} async-done(((f32[32,1,384]{2,1,0:T(1,128)}), f32[32,1,384]{2,1,0:T(1,128)S(1)}, u32[]{:S(2)}, u32[]{:S(2)}) %all-to-all-start) | async-done | bytes 49184 | tf_op jit(solution)/shard_map/all_to_all | solution.py:32
  25.4 1.3 %shard_map.60 = f32[32,8,96]{2,1,0:T(8,128)S(1)} custom-call(f32[32,384]{1,0:T(8,128)S(1)} %bitcast.4, bf16[16,256,384]{2,1,0:T(8,128)(2,1)S(1)} %shard_map.59.split_ref), custom_call_target="tpu_custom_call" | custom-call | tf_op jit(solution)/shard_map/pallas_call | solution.py:42
  26.7 11.4 %all_to_all.15.parts_ref = f32[32,8,96]{2,1,0:T(8,128)S(1)} all-to-all(f32[32,8,96]{2,1,0:T(8,128)S(1)} %shard_map.60), channel_id=1, replica_groups={{26,27,24,25,30,31,28,29,18,19,16,17,22,23,20,21,10,11,8,9,14,15,12,13,..., dimensions={0} | all-to-all | bytes 196608 | tf_op jit(solution)/shard_map/all_to_all | solution.py:32
  38.1 1.1 %shard_map.61 = (f32[16,4,84]{2,1,0:T(4,128)S(1)}, f32[16,24]{1,0:T(8,128)S(1)}) custom-call(f32[32,8,96]{2,1,0:T(8,128)S(1)} %all_to_all.15.parts_ref), custom_call_target="tpu_custom_call" | custom-call | tf_op jit(solution)/shard_map/pallas_call | solution.py:42
  39.2 13.9 %all_to_all.16.grams_ref = f32[16,4,84]{2,1,0:T(4,128)S(1)} all-to-all(f32[16,4,84]{2,1,0:T(4,128)S(1)} %get-tuple-element.8), channel_id=1, replica_groups={{288,320,352,384,416,448,480,0,32,64,96,128,160,192,224,256},{289,321,3..., dimensions={0} | all-to-all | bytes 43008 | tf_op jit(solution)/shard_map/all_to_all | solution.py:32
  53.1 0.9 %shard_map.62 = (f32[16,24]{1,0:T(8,128)}, f32[1,24]{1,0:T(1,128)}, f32[24,24]{1,0:T(8,128)}) custom-call(f32[16,4,84]{2,1,0:T(4,128)S(1)} %all_to_all.16.grams_ref, f32[16,24]{1,0:T(8,128)S(1)} %get-tuple-element.9.updated_ref), custom_call_target="tpu_custom_call" | custom-call | tf_op jit(solution)/shard_map/pallas_call | solution.py:42
  (1 shorter events, 0.0 us)
Async XLA Ops:
  2.1 23.4 %all-to-all-start = ((f32[32,1,384]{2,1,0:T(1,128)}), f32[32,1,384]{2,1,0:T(1,128)S(1)}, u32[]{:S(2)}, u32[]{:S(2)}) async-start(f32[32,1,384]{2,1,0:T(1,128)} %shard_map.58), calls=%async_computation | async-start | bytes 98304 | tf_op jit(solution)/shard_map/all_to_all | solution.py:32
  20.1 1.6 %copy-start = (f32[16,256,128]{2,1,0:T(8,128)S(1)}, f32[16,256,128]{2,1,0:T(8,128)}, u32[]{:S(2)}) copy-start(f32[16,256,128]{2,1,0:T(8,128)} %tensor_ref.1) | copy-start | bytes 6291460

commit v8 on v7

--- a/solution.py
+++ b/solution.py
@@ -50,14 +50,18 @@
     )(*operands)
 
 
-def pack_kernel(two_hbm, three_hbm, out_ref, two_ref, three_ref, arrived):
+def pack_kernel(two_hbm, three_hbm, tensor_hbm, out_ref, tensor_ref, two_ref, three_ref, arrived):
     copies = [
         pltpu.make_async_copy(two_hbm, two_ref, arrived.at[0]),
         pltpu.make_async_copy(three_hbm, three_ref, arrived.at[1]),
     ]
-    for copy in copies:
+    half = tensor_ref.shape[0] // 2
+    for at in range(2):
+        rows = pl.ds(at * half, half)
+        copies.append(pltpu.make_async_copy(tensor_hbm.at[rows], tensor_ref.at[rows], arrived.at[2 + at]))
+    for copy in reversed(copies):
         copy.start()
-    for copy in copies:
+    for copy in copies[:2]:
         copy.wait()
     rank = two_ref.shape[-1]
     rows = [two_ref[0, r : r + 1, :] for r in range(two_ref.shape[1])]
@@ -71,6 +75,8 @@
         at = start + rank
     pieces.append(jnp.zeros((1, out_ref.shape[-1] - at), jnp.float32))
     out_ref[...] = jnp.broadcast_to(jnp.concatenate(pieces, axis=1)[None], out_ref.shape)
+    for copy in copies[2:]:
+        copy.wait()
 
 
 def parts_of(thrice, rank):
@@ -98,22 +104,8 @@
     return fold_gram(full, rank)
 
 
-def split_kernel(tensor_ref, split_ref):
-    width = tensor_ref.shape[-1]
-
-    @pl.loop(0, tensor_ref.shape[0])
-    def _(row):
-        cells = tensor_ref[row]
-        high = cells.astype(jnp.bfloat16)
-        rest = cells - high.astype(jnp.float32)
-        middle = rest.astype(jnp.bfloat16)
-        split_ref[row, :, :width] = high
-        split_ref[row, :, width : 2 * width] = middle
-        split_ref[row, :, 2 * width :] = (rest - middle.astype(jnp.float32)).astype(jnp.bfloat16)
-
-
 def contract_kernel(
-    gathered_ref, split_ref, out_ref, two_ref, three_ref, sums_ref,
+    gathered_ref, tensor_ref, out_ref, two_ref, three_ref, sums_ref,
     gram_two_ref, gram_three_ref, *, rank, orders
 ):
     cores, chips = map(len, orders)
@@ -139,8 +131,15 @@
     two = two_ref[...]
     parts_three = parts_of(three_ref[...], rank)
     stacked = jnp.concatenate([parts_three, parts_three, parts_three], axis=0)
-    for row in range(split_ref.shape[0]):
-        through = jnp.dot(split_ref[row], stacked, preferred_element_type=jnp.float32)
+    for row in range(tensor_ref.shape[0]):
+        cells = tensor_ref[row]
+        high = cells.astype(jnp.bfloat16)
+        rest = cells - high.astype(jnp.float32)
+        middle = rest.astype(jnp.bfloat16)
+        low = (rest - middle.astype(jnp.float32)).astype(jnp.bfloat16)
+        through = jnp.dot(
+            jnp.concatenate([high, middle, low], axis=1), stacked, preferred_element_type=jnp.float32
+        )
         sums_ref[row : row + 1, :] = jnp.sum(through * two, axis=0, keepdims=True)
     partial = fold_lanes(sums_ref[...], rank).T
     gram_two_ref[...] = gram_of_parts(parts_of(two, rank), rank)
@@ -274,8 +273,8 @@
 
 def per_device(tensor, second_factor, third_factor):
     f32 = jnp.float32
-    second_factor, third_factor = (
-        pltpu.with_memory_space_constraint(v, pltpu.HBM) for v in (second_factor, third_factor)
+    tensor, second_factor, third_factor = (
+        pltpu.with_memory_space_constraint(v, pltpu.HBM) for v in (tensor, second_factor, third_factor)
     )
     rank = second_factor.shape[-1]
     chips, cores = lax.axis_size("z"), lax.axis_size("core")
@@ -287,17 +286,18 @@
     width = -(-(lane_start(slots - 1, rank) + rank) // LANES) * LANES
     tiles = rank // SUBLANES
 
-    packed = call(
+    packed, tensor = call(
         pack_kernel,
-        jax.ShapeDtypeStruct((members, 1, width), f32),
+        (jax.ShapeDtypeStruct((members, 1, width), f32), jax.ShapeDtypeStruct(tensor.shape, f32)),
         [
             pltpu.VMEM(second_factor.shape, f32),
             pltpu.VMEM(third_factor.shape, f32),
-            pltpu.SemaphoreType.DMA((2,)),
+            pltpu.SemaphoreType.DMA((4,)),
         ],
         second_factor,
         third_factor,
-        fetched=(0, 1),
+        tensor,
+        fetched=(0, 1, 2),
     )
     cores_order = counted_from(cores - 1, cores)
     rows_order = (cores_order, upper_first(5 * chips // 8, chips))
@@ -309,13 +309,6 @@
     chips_order = (counted_from(chips // 2 + 1, chips),)
     gathered = exchange(packed, ("core", "z"), rows_order).reshape(members, width)
 
-    split = call(
-        split_kernel,
-        jax.ShapeDtypeStruct((*tensor.shape[:2], 3 * tensor.shape[2]), jnp.bfloat16),
-        [],
-        tensor,
-        cost=pl.CostEstimate(flops=5 * tensor.size, bytes_accessed=10 * tensor.size, transcendentals=0),
-    )
     messages = call(
         functools.partial(contract_kernel, rank=rank, orders=rows_order),
         jax.ShapeDtypeStruct((cores * groups_two * groups_three, SUBLANES, tiles * rows + 2 * rank), f32),
@@ -327,7 +320,7 @@
             pltpu.VMEM((rank, rank), f32),
         ],
         gathered,
-        split,
+        tensor,
     )
     parts = exchange(messages, ("core", "ja", "ka"), plane_order)
 

time: 54.2 us -> 54.2 us (level)
  blocking collectives: 25.3 us -> 48.4 us
  starting transfers between devices: 18 us -> 0 us
  waiting for transfers between devices: 3.09 us -> 0 us
  local copies, waits for them, and re-layouts: 1.59 us -> 0.01 us
    all_to_all x2 -> x3, blocking collectives: 25.3 us -> 48.4 us  [exchange(): lax.all_to_all(copies, axes, 0, 0, tiled=True, axis_index_groups=[listed])]
    all_to_all x1 -> x0, starting transfers between devices: 18 us -> none  [exchange(): lax.all_to_all(copies, axes, 0, 0, tiled=True, axis_index_groups=[listed])]
    all_to_all x1 -> x0, waiting for transfers between devices: 3.09 us -> none  [exchange(): lax.all_to_all(copies, axes, 0, 0, tiled=True, axis_index_groups=[listed])]
    unnamed x3 -> x1, local copies, waits for them, and re-layouts: 1.59 us -> 0.01 us
    pallas_call x5 -> x4, Pallas kernels: 5.3 us -> 4.85 us  [call(): pl.pallas_call(kernel, out_shape=out_shape, in_specs=[hbm if at in fetche...]
  transfers between devices with their start and end apart: 1 -> 0, of which waited for: 1 -> 0; matrix products, arithmetic and copies ran while one was open for 0% -> 0% of each run, Pallas kernels for 1% -> 0%
where the time goes in v8:
time: 54.2 us; the launch traced here: 53.9 us
  blocking collectives  48.4 us (89%)
  Pallas kernels  4.85 us (9%)
  between operations  0.65 us (1%)
    all_to_all x3, blocking collectives, exchange(): lax.all_to_all(copies, axes, 0, 0, tiled=True, axis_index_groups=[listed])  48.4 us
    pallas_call x4, Pallas kernels, call(): pl.pallas_call(kernel, out_shape=out_shape, in_specs=[hbm if at in fetche...  4.85 us

profile of v8, /device:TPU:1, one launch (start us, length us, event | category | flops | bytes accessed | tf_op | source)
XLA Modules:
  0.0 53.9 jit_solution(4278845913851763882)
XLA Ops:
  0.6 1.6 %shard_map.58 = (f32[32,1,384]{2,1,0:T(1,128)S(1)}, f32[16,256,128]{2,1,0:T(8,128)S(1)}) custom-call(f32[1,8,24]{2,1,0:T(8,128)} %two_hbm.1, f32[1,4,24]{2,1,0:T(4,128)} %three_hbm.1, f32[16,256,128]{2,1,0:T(8,128)} %tensor_hbm.1), custom_call_target="tpu_custom_call" | custom-call | tf_op jit(solution)/shard_map/pallas_call | solution.py:42
  2.2 23.2 %all_to_all.15 = f32[32,1,384]{2,1,0:T(1,128)S(1)} all-to-all(f32[32,1,384]{2,1,0:T(1,128)S(1)} %get-tuple-element.10), channel_id=1, replica_groups={{336,368,400,432,464,496,272,304,16,48,80,112,144,176,208,240,320,352,3..., dimensions={0} | all-to-all | bytes 98304 | tf_op jit(solution)/shard_map/all_to_all | solution.py:32
  25.4 1.3 %shard_map.59 = f32[32,8,96]{2,1,0:T(8,128)S(1)} custom-call(f32[32,384]{1,0:T(8,128)S(1)} %bitcast.4, f32[16,256,128]{2,1,0:T(8,128)S(1)} %get-tuple-element.11.tensor_ref), custom_call_target="tpu_custom_call" | custom-call | tf_op jit(solution)/shard_map/pallas_call | solution.py:42
  26.7 11.4 %all_to_all.16.parts_ref = f32[32,8,96]{2,1,0:T(8,128)S(1)} all-to-all(f32[32,8,96]{2,1,0:T(8,128)S(1)} %shard_map.59), channel_id=1, replica_groups={{26,27,24,25,30,31,28,29,18,19,16,17,22,23,20,21,10,11,8,9,14,15,12,13,..., dimensions={0} | all-to-all | bytes 196608 | tf_op jit(solution)/shard_map/all_to_all | solution.py:32
  38.1 1.1 %shard_map.60 = (f32[16,4,84]{2,1,0:T(4,128)S(1)}, f32[16,24]{1,0:T(8,128)S(1)}) custom-call(f32[32,8,96]{2,1,0:T(8,128)S(1)} %all_to_all.16.parts_ref), custom_call_target="tpu_custom_call" | custom-call | tf_op jit(solution)/shard_map/pallas_call | solution.py:42
  39.2 13.9 %all_to_all.17.grams_ref = f32[16,4,84]{2,1,0:T(4,128)S(1)} all-to-all(f32[16,4,84]{2,1,0:T(4,128)S(1)} %get-tuple-element.12), channel_id=1, replica_groups={{288,320,352,384,416,448,480,0,32,64,96,128,160,192,224,256},{289,321,3..., dimensions={0} | all-to-all | bytes 43008 | tf_op jit(solution)/shard_map/all_to_all | solution.py:32
  53.1 0.9 %shard_map.61 = (f32[16,24]{1,0:T(8,128)}, f32[1,24]{1,0:T(1,128)}, f32[24,24]{1,0:T(8,128)}) custom-call(f32[16,4,84]{2,1,0:T(4,128)S(1)} %all_to_all.17.grams_ref, f32[16,24]{1,0:T(8,128)S(1)} %get-tuple-element.13.updated_ref), custom_call_target="tpu_custom_call" | custom-call | tf_op jit(solution)/shard_map/pallas_call | solution.py:42
  (1 shorter events, 0.0 us)

commit v9 on v8

--- a/solution.py
+++ b/solution.py
@@ -13,6 +13,7 @@
 LANES = 128
 SUBLANES = 8
 QUAD = 4
+ROWS_AT_ONCE = 8
 BLOCK = 12
 VMEM_BYTES = 8 * 2**20
 
@@ -131,16 +132,16 @@
     two = two_ref[...]
     parts_three = parts_of(three_ref[...], rank)
     stacked = jnp.concatenate([parts_three, parts_three, parts_three], axis=0)
-    for row in range(tensor_ref.shape[0]):
-        cells = tensor_ref[row]
+    for row in range(0, tensor_ref.shape[0], ROWS_AT_ONCE):
+        cells = tensor_ref[row : row + ROWS_AT_ONCE].reshape(-1, tensor_ref.shape[2])
         high = cells.astype(jnp.bfloat16)
         rest = cells - high.astype(jnp.float32)
         middle = rest.astype(jnp.bfloat16)
         low = (rest - middle.astype(jnp.float32)).astype(jnp.bfloat16)
         through = jnp.dot(
             jnp.concatenate([high, middle, low], axis=1), stacked, preferred_element_type=jnp.float32
-        )
-        sums_ref[row : row + 1, :] = jnp.sum(through * two, axis=0, keepdims=True)
+        ).reshape(ROWS_AT_ONCE, *two.shape)
+        sums_ref[row : row + ROWS_AT_ONCE, :] = jnp.sum(through * two[None], axis=1)
     partial = fold_lanes(sums_ref[...], rank).T
     gram_two_ref[...] = gram_of_parts(parts_of(two, rank), rank)
     gram_three_ref[...] = gram_of_parts(parts_three, rank)

time: 54.2 us -> 54.2 us (level)
  no operation moved by 1% of the time
where the time goes in v9:
time: 54.2 us; the launch traced here: 53.9 us
  blocking collectives  48.4 us (89%)
  Pallas kernels  4.87 us (9%)
  between operations  0.65 us (1%)
    all_to_all x3, blocking collectives, exchange(): lax.all_to_all(copies, axes, 0, 0, tiled=True, axis_index_groups=[listed])  48.4 us
    pallas_call x4, Pallas kernels, call(): pl.pallas_call(kernel, out_shape=out_shape, in_specs=[hbm if at in fetche...  4.87 us

profile of v9, /device:TPU:1, one launch (start us, length us, event | category | flops | bytes accessed | tf_op | source)
XLA Modules:
  0.0 53.9 jit_solution(8389600895677658768)
XLA Ops:
  0.6 1.6 %shard_map.58 = (f32[32,1,384]{2,1,0:T(1,128)S(1)}, f32[16,256,128]{2,1,0:T(8,128)S(1)}) custom-call(f32[1,8,24]{2,1,0:T(8,128)} %two_hbm.1, f32[1,4,24]{2,1,0:T(4,128)} %three_hbm.1, f32[16,256,128]{2,1,0:T(8,128)} %tensor_hbm.1), custom_call_target="tpu_custom_call" | custom-call | tf_op jit(solution)/shard_map/pallas_call | solution.py:43
  2.2 23.2 %all_to_all.15 = f32[32,1,384]{2,1,0:T(1,128)S(1)} all-to-all(f32[32,1,384]{2,1,0:T(1,128)S(1)} %get-tuple-element.10), channel_id=1, replica_groups={{336,368,400,432,464,496,272,304,16,48,80,112,144,176,208,240,320,352,3..., dimensions={0} | all-to-all | bytes 98304 | tf_op jit(solution)/shard_map/all_to_all | solution.py:33
  25.4 1.4 %shard_map.59 = f32[32,8,96]{2,1,0:T(8,128)S(1)} custom-call(f32[32,384]{1,0:T(8,128)S(1)} %bitcast.4, f32[16,256,128]{2,1,0:T(8,128)S(1)} %get-tuple-element.11.tensor_ref), custom_call_target="tpu_custom_call" | custom-call | tf_op jit(solution)/shard_map/pallas_call | solution.py:43
  26.7 11.4 %all_to_all.16.parts_ref = f32[32,8,96]{2,1,0:T(8,128)S(1)} all-to-all(f32[32,8,96]{2,1,0:T(8,128)S(1)} %shard_map.59), channel_id=1, replica_groups={{26,27,24,25,30,31,28,29,18,19,16,17,22,23,20,21,10,11,8,9,14,15,12,13,..., dimensions={0} | all-to-all | bytes 196608 | tf_op jit(solution)/shard_map/all_to_all | solution.py:33
  38.1 1.1 %shard_map.60 = (f32[16,4,84]{2,1,0:T(4,128)S(1)}, f32[16,24]{1,0:T(8,128)S(1)}) custom-call(f32[32,8,96]{2,1,0:T(8,128)S(1)} %all_to_all.16.parts_ref), custom_call_target="tpu_custom_call" | custom-call | tf_op jit(solution)/shard_map/pallas_call | solution.py:43
  39.2 13.9 %all_to_all.17.grams_ref = f32[16,4,84]{2,1,0:T(4,128)S(1)} all-to-all(f32[16,4,84]{2,1,0:T(4,128)S(1)} %get-tuple-element.12), channel_id=1, replica_groups={{288,320,352,384,416,448,480,0,32,64,96,128,160,192,224,256},{289,321,3..., dimensions={0} | all-to-all | bytes 43008 | tf_op jit(solution)/shard_map/all_to_all | solution.py:33
  53.1 0.9 %shard_map.61 = (f32[16,24]{1,0:T(8,128)}, f32[1,24]{1,0:T(1,128)}, f32[24,24]{1,0:T(8,128)}) custom-call(f32[16,4,84]{2,1,0:T(4,128)S(1)} %all_to_all.17.grams_ref, f32[16,24]{1,0:T(8,128)S(1)} %get-tuple-element.13.updated_ref), custom_call_target="tpu_custom_call" | custom-call | tf_op jit(solution)/shard_map/pallas_call | solution.py:43
  (1 shorter events, 0.0 us)

commit v10 on v9

--- a/solution.py
+++ b/solution.py
@@ -13,7 +13,7 @@
 LANES = 128
 SUBLANES = 8
 QUAD = 4
-ROWS_AT_ONCE = 8
+ROWS_AT_ONCE = 16
 BLOCK = 12
 VMEM_BYTES = 8 * 2**20
 

time: 54.2 us -> 54.2 us (level)
  no operation moved by 1% of the time
where the time goes in v10:
time: 54.2 us; the launch traced here: 54 us
  blocking collectives  48.4 us (89%)
  Pallas kernels  4.92 us (9%)
  between operations  0.65 us (1%)
    all_to_all x3, blocking collectives, exchange(): lax.all_to_all(copies, axes, 0, 0, tiled=True, axis_index_groups=[listed])  48.4 us
    pallas_call x4, Pallas kernels, call(): pl.pallas_call(kernel, out_shape=out_shape, in_specs=[hbm if at in fetche...  4.92 us

profile of v10, /device:TPU:1, one launch (start us, length us, event | category | flops | bytes accessed | tf_op | source)
XLA Modules:
  0.0 54.0 jit_solution(14103397077592494567)
XLA Ops:
  0.6 1.6 %shard_map.58 = (f32[32,1,384]{2,1,0:T(1,128)S(1)}, f32[16,256,128]{2,1,0:T(8,128)S(1)}) custom-call(f32[1,8,24]{2,1,0:T(8,128)} %two_hbm.1, f32[1,4,24]{2,1,0:T(4,128)} %three_hbm.1, f32[16,256,128]{2,1,0:T(8,128)} %tensor_hbm.1), custom_call_target="tpu_custom_call" | custom-call | tf_op jit(solution)/shard_map/pallas_call | solution.py:43
  2.2 23.2 %all_to_all.15 = f32[32,1,384]{2,1,0:T(1,128)S(1)} all-to-all(f32[32,1,384]{2,1,0:T(1,128)S(1)} %get-tuple-element.10), channel_id=1, replica_groups={{336,368,400,432,464,496,272,304,16,48,80,112,144,176,208,240,320,352,3..., dimensions={0} | all-to-all | bytes 98304 | tf_op jit(solution)/shard_map/all_to_all | solution.py:33
  25.4 1.4 %shard_map.59 = f32[32,8,96]{2,1,0:T(8,128)S(1)} custom-call(f32[32,384]{1,0:T(8,128)S(1)} %bitcast.4, f32[16,256,128]{2,1,0:T(8,128)S(1)} %get-tuple-element.11.tensor_ref), custom_call_target="tpu_custom_call" | custom-call | tf_op jit(solution)/shard_map/pallas_call | solution.py:43
  26.8 11.4 %all_to_all.16.parts_ref = f32[32,8,96]{2,1,0:T(8,128)S(1)} all-to-all(f32[32,8,96]{2,1,0:T(8,128)S(1)} %shard_map.59), channel_id=1, replica_groups={{26,27,24,25,30,31,28,29,18,19,16,17,22,23,20,21,10,11,8,9,14,15,12,13,..., dimensions={0} | all-to-all | bytes 196608 | tf_op jit(solution)/shard_map/all_to_all | solution.py:33
  38.2 1.1 %shard_map.60 = (f32[16,4,84]{2,1,0:T(4,128)S(1)}, f32[16,24]{1,0:T(8,128)S(1)}) custom-call(f32[32,8,96]{2,1,0:T(8,128)S(1)} %all_to_all.16.parts_ref), custom_call_target="tpu_custom_call" | custom-call | tf_op jit(solution)/shard_map/pallas_call | solution.py:43
  39.3 13.9 %all_to_all.17.grams_ref = f32[16,4,84]{2,1,0:T(4,128)S(1)} all-to-all(f32[16,4,84]{2,1,0:T(4,128)S(1)} %get-tuple-element.12), channel_id=1, replica_groups={{288,320,352,384,416,448,480,0,32,64,96,128,160,192,224,256},{289,321,3..., dimensions={0} | all-to-all | bytes 43008 | tf_op jit(solution)/shard_map/all_to_all | solution.py:33
  53.1 0.9 %shard_map.61 = (f32[16,24]{1,0:T(8,128)}, f32[1,24]{1,0:T(1,128)}, f32[24,24]{1,0:T(8,128)}) custom-call(f32[16,4,84]{2,1,0:T(4,128)S(1)} %all_to_all.17.grams_ref, f32[16,24]{1,0:T(8,128)S(1)} %get-tuple-element.13.updated_ref), custom_call_target="tpu_custom_call" | custom-call | tf_op jit(solution)/shard_map/pallas_call | solution.py:43
  (1 shorter events, 0.0 us)
